TPU v7x, 128 devices: a whole 4x4x4 slice. The times are simulated.
128 devices in a mesh: leaf: 2 (over core), wide: 64 (over z, y, x).
Axes of the slice: x: 4, y: 4, z: 4, core: 2. Of those that a mesh axis runs over, the one named last changes fastest.
Arguments:
- drop_sides: float32 [96, 393216], P(None, ('leaf', 'wide')), may hold values from -6 to 6
- super_index: int32 [393216], P(('leaf', 'wide')), may hold values from 0 to 393215, as said below
- low_inverse: float32 [1024, 384, 384], P(('leaf', 'wide')), may hold values from -2 to 2
- coupling: bfloat16 [393216, 768], P(('leaf', 'wide')), may hold values from -0.0390625 to 0.0390625
- top_sides: float32 [96, 768], P(None, 'leaf'), may hold values from -6 to 6
- top_inverse: float32 [2, 384, 384], P('leaf'), may hold values from -2 to 2
- top_coupling: bfloat16 [2, 2, 384, 384], P(None, 'leaf'), may hold values from -0.21875 to 0.21875
Outputs:
- drop_solution: float32 [96, 393216], P(None, ('leaf', 'wide'))
- top_solution: float32 [96, 768], P(None, 'leaf')
Inputs may be any that keep to these rules, and one draw needn't show every extreme that they name: `super_index`: A permutation that keeps each row within its leaf group's 3072 * 64 rows. Each device sends exactly 48 rows to every device of its group, itself included.
All inputs are finite; a program needn't handle non-finite values.
Results may differ from a plain program's by a relative error of at most 0.003.
Values may be sent and summed in bfloat16 or wider, within the bound.
A program may use at most 64 MiB of HBM per device.

v0:
```python
import jax
import jax.numpy as jnp
from jax import lax
from jax.sharding import PartitionSpec as P


def spread(shard, axis, root):
    mine = lax.axis_index(axis) == root
    return lax.psum(jnp.where(mine, shard, jnp.zeros_like(shard)), axis)


def shards(drop_sides, super_index, low_inverse, coupling, top_sides, top_inverse, top_coupling):
    side_count = drop_sides.shape[0]
    row_count = drop_sides.shape[1]
    node_count = low_inverse.shape[0]
    width = low_inverse.shape[1]
    top_count = top_coupling.shape[0]
    wide_count = lax.axis_size("wide")
    capacity = row_count // wide_count
    leaf_index = lax.axis_index("leaf")
    local = super_index - leaf_index * wide_count * row_count
    target = local // row_count
    position = local % row_count
    onehot = (target[:, None] == jnp.arange(wide_count, dtype=jnp.int32)[None, :]).astype(jnp.int32)
    before = jnp.cumsum(onehot, axis=0) - onehot
    ranking = jnp.sum(before * onehot, axis=1)
    slots = target * capacity + ranking
    outgoing = (
        jnp.zeros((side_count, wide_count * capacity), jnp.float32).at[:, slots].set(drop_sides)
    )
    places = (
        jnp.full((wide_count * capacity,), float(row_count), jnp.float32)
        .at[slots]
        .set(position.astype(jnp.float32))
    )
    arrived, arrived_places = (
        lax.all_to_all(
            outgoing.reshape(side_count, wide_count, capacity),
            "wide",
            split_axis=1,
            concat_axis=1,
            tiled=True,
        ),
        lax.all_to_all(
            places.reshape(1, wide_count, capacity), "wide", split_axis=1, concat_axis=1, tiled=True
        ),
    )
    where_from = arrived_places.reshape(-1).astype(jnp.int32)
    super_sides = (
        jnp.zeros((side_count, row_count), jnp.float32)
        .at[:, where_from]
        .set(arrived.reshape(side_count, -1), mode="drop")
    )
    low_solved = jnp.einsum(
        "rsb,sbc->rsc",
        super_sides.reshape(side_count, node_count, width),
        low_inverse,
        precision=lax.Precision.HIGHEST,
    ).reshape(side_count, row_count)
    low_half = low_solved.astype(jnp.bfloat16)
    blocked = coupling.reshape(row_count, top_count, width)
    partial_sum = jnp.einsum("rl,lnb->nrb", low_half, blocked, preferred_element_type=jnp.float32)
    totals = lax.psum(partial_sum, ("leaf", "wide"))
    own_sum = lax.dynamic_index_in_dim(totals, leaf_index, 0, keepdims=False)
    top_residual = top_sides - own_sum
    own_inverse = top_inverse[0]
    own_column = top_coupling[:, 0]
    gathered = jnp.zeros((side_count, width), jnp.float32)
    top_solved = jnp.zeros((side_count, width), jnp.float32)
    for column in range(top_count):
        candidate = jnp.dot(top_residual - gathered, own_inverse, precision=lax.Precision.HIGHEST)
        top_solved = jnp.where(leaf_index == column, candidate, top_solved)
        if column + 1 < top_count:
            solved = spread(candidate.astype(jnp.bfloat16), "leaf", column)
            gathered = jnp.dot(solved, own_column[column], preferred_element_type=jnp.float32)
    top_answer = jnp.zeros((side_count, width), jnp.float32)
    answer_half = jnp.zeros((side_count, width), jnp.bfloat16)
    for column in range(top_count - 1, -1, -1):
        current = top_solved
        if column + 1 < top_count:
            term = lax.dot_general(
                answer_half,
                own_column[column],
                (((1,), (1,)), ((), ())),
                preferred_element_type=jnp.float32,
            )
            current = top_solved - lax.psum(term, "leaf")
        candidate = lax.dot_general(
            current, own_inverse, (((1,), (1,)), ((), ())), precision=lax.Precision.HIGHEST
        )
        top_answer = jnp.where(leaf_index == column, candidate, top_answer)
        answer_half = top_answer.astype(jnp.bfloat16)
    low_term = jnp.einsum(
        "nrb,lnb->rl",
        lax.all_gather(answer_half[None], "leaf", axis=0, tiled=True),
        blocked,
        preferred_element_type=jnp.float32,
    )
    low_solution = jnp.einsum(
        "rsb,scb->rsc",
        (low_solved - low_term).reshape(side_count, node_count, width),
        low_inverse,
        precision=lax.Precision.HIGHEST,
    ).reshape(side_count, row_count)
    outgoing_back = low_solution[:, jnp.minimum(where_from, row_count - 1)]
    returned = lax.all_to_all(
        outgoing_back.reshape(side_count, wide_count, capacity),
        "wide",
        split_axis=1,
        concat_axis=1,
        tiled=True,
    )
    drop_solution = returned.reshape(side_count, -1)[:, slots]
    return (drop_solution, top_answer)


def solution(mesh):
    placed = (
        P(None, ("leaf", "wide")),
        P(("leaf", "wide")),
        P(("leaf", "wide"), None, None),
        P(("leaf", "wide"), None),
        P(None, "leaf"),
        P("leaf", None, None),
        P(None, "leaf", None, None),
    )
    return jax.shard_map(
        shards,
        mesh=mesh,
        in_specs=placed,
        out_specs=(P(None, ("leaf", "wide")), P(None, "leaf")),
        check_vma=False,
    )
```

profile of v0, /device:TPU:0, one launch (start us, length us, event | category | flops | bytes accessed | tf_op | source)
XLA Modules:
  0.0 387.8 jit_solution(7325886831637015324)
XLA Ops:
  8.0 18.3 %reduce-window.6 = s32[64,24,128]{2,1,0:T(8,128)S(1)} reduce-window(s32[64,24,128]{2,1,0:T(8,128)S(1)} %fusion.24, s32[]{:T(128)} %constant.47.clone.1), window={size=1x1x128 pad=0_0x0_0x127_0}, to_apply=%region_0.1 | reduce-window | flops 24969216 | bytes 1572868 | tf_op jit(solution)/shard_map/reduce-window
  27.8 11.8 %scatter_custom_fusion = f32[3072]{0:T(1024)S(1)} fusion(s32[3072]{0:T(1024)S(1)} %get-tuple-element.9, f32[3072]{0:T(1024)S(1)} %get-tuple-element.12, f32[]{:T(128)} %constant.24.clone.1), kind=kCustom, calls=%fused_computation.60 | custom fusion | bytes 12292 | tf_op jit(solution)/shard_map/scatter | solution.py:34
  40.3 11.5 %all-to-all-start = ((f32[1,64,48]{2,0,1:T(1,128)}), f32[1,64,48]{2,0,1:T(1,128)S(1)}, u32[]{:S(2)}, u32[]{:S(2)}) async-start(f32[1,64,48]{2,0,1:T(1,128)} %bitcast.4), calls=%async_computation | async-start | bytes 65536 | tf_op jit(solution)/shard_map/all_to_all | solution.py:44
  52.3 9.3 %scatter_custom_fusion.1 = f32[96,3072]{0,1:T(8,128)} fusion(s32[3072]{0:T(1024)S(1)} %get-tuple-element.9, f32[3072,96]{1,0:T(8,128)S(1)} %copy.30, f32[]{:T(128)} %constant.20.clone.1), kind=kCustom, calls=%fused_computation.30 | custom fusion | bytes 1179652 | tf_op jit(solution)/shard_map/scatter | solution.py:29
  61.6 10.3 %all-to-all-start.1 = ((f32[96,64,48]{0,2,1:T(8,128)}), f32[96,64,48]{0,2,1:T(8,128)S(1)}, u32[]{:S(2)}, u32[]{:S(2)}) async-start(f32[96,64,48]{0,2,1:T(8,128)} %bitcast.7), calls=%async_computation.1 | async-start | bytes 3145728 | tf_op jit(solution)/shard_map/all_to_all | solution.py:37
  72.2 23.6 %all-to-all-done.1 = f32[96,64,48]{0,2,1:T(8,128)S(1)} async-done(((f32[96,64,48]{0,2,1:T(8,128)}), f32[96,64,48]{0,2,1:T(8,128)S(1)}, u32[]{:S(2)}, u32[]{:S(2)}) %all-to-all-start.1) | async-done | bytes 1179680 | tf_op jit(solution)/shard_map/all_to_all | solution.py:37
  95.8 1.2 copy-done.1
  97.0 8.8 %scatter_custom_fusion.2 = f32[96,3072]{0,1:T(8,128)S(1)} fusion(s32[3072]{0:T(1024)S(1)} %bitcast.116, f32[3072,96]{1,0:T(8,128)} %bitcast.109, f32[]{:T(128)} %constant.20.clone.1), kind=kCustom, calls=%fused_computation.28 | custom fusion | bytes 1180160 | tf_op jit(solution)/shard_map/scatter | solution.py:52
  105.8 5.2 %bitcast_convert_fusion = (bf16[96,8,384]{2,0,1:T(8,128)(2,1)S(1)}, f32[8,96,384]{2,1,0:T(8,128)S(1)}) fusion(f32[96,8,384]{0,2,1:T(8,128)S(1)} %bitcast.100, f32[8,384,384]{2,1,0:T(8,128)} %param.9), kind=kOutput, calls=%fused_computation.16 | convolution fusion | flops 1359249408 | bytes 7667712 | tf_op jit(solution)/shard_map/rsb,sbc->rsc/dot_general | solution.py:54
  111.5 4.0 %fusion.14 = f32[2,96,384]{2,1,0:T(8,128)} fusion(bf16[96,3072,1]{1,0,2:T(8,128)(2,1)S(1)} %reshape.145, bf16[384,2,8,384]{3,2,1,0:T(8,128)(2,1)} %bitcast.105), kind=kOutput, calls=%fused_computation.17 | convolution fusion | flops 452984832 | bytes 5603328 | tf_op jit(solution)/shard_map/rl,lnb->nrb/dot_general | solution.py:62
  115.5 138.3 %all-reduce.4.cloned.1.call-done = f32[2,96,384]{2,1,0:T(8,128)} async-done(((f32[2,96,384]{2,1,0:T(8,128)}), f32[2,96,384]{2,1,0:T(8,128)}) %all-reduce.4.cloned.1.call-update) | async-done | bytes 294928 | tf_op jit(solution)/shard_map/psum | solution.py:63
  253.8 2.1 convert_select_fusion
  256.1 21.7 %all-reduce.6.cloned.1.call-done = bf16[96,384]{1,0:T(8,128)(2,1)} async-done(((bf16[96,384]{1,0:T(8,128)(2,1)}), bf16[96,384]{1,0:T(8,128)(2,1)}) %all-reduce.6.cloned.1.call-update) | async-done | bytes 73744 | tf_op jit(solution)/shard_map/psum | solution.py:9
  277.9 1.1 convolution_subtract_fusion
  280.3 0.9 fusion.30
  281.3 24.9 %all-reduce.8.cloned.1.call-done = f32[96,384]{1,0:T(8,128)} async-done(((f32[96,384]{1,0:T(8,128)}), f32[96,384]{1,0:T(8,128)}) %all-reduce.8.cloned.1.call-update) | async-done | bytes 147472 | tf_op jit(solution)/shard_map/psum | solution.py:87
  306.2 2.3 fusion.42
  308.5 1.9 all-gather
  310.4 3.9 fusion.9
  314.3 6.7 %convolution_bitcast_fusion = f32[96,8,384]{2,0,1:T(8,128)S(1)} fusion(f32[8,384,384]{2,1,0:T(8,128)} %param.9, f32[12,8,8,384]{3,2,1,0:T(8,128)S(1)} %bitcast.103), kind=kOutput, calls=%fused_computation.13 | convolution fusion | flops 1358954496 | bytes 7077888 | tf_op jit(solution)/shard_map/rsb,scb->rsc/dot_general | solution.py:99
  321.4 10.8 %gather_fusion = f32[3072,96]{1,0:T(8,128)} fusion(f32[96,3072]{0,1:T(8,128)S(1)} %bitcast.99, s32[3072]{0:T(1024)S(1)} %broadcast_clamp_fusion.1), kind=kCustom, calls=%fused_computation | custom fusion | bytes 2371584 | tf_op jit(solution)/shard_map/gather | solution.py:105
  332.3 35.3 %all_to_all.15 = f32[96,64,48]{0,2,1:T(8,128)S(1)} all-to-all(f32[96,64,48]{0,2,1:T(8,128)} %bitcast.101), channel_id=1, replica_groups=mesh['leaf'=2,'wide'=64] {'wide'}, dimensions={1} | all-to-all | bytes 2359296 | tf_op jit(solution)/shard_map/all_to_all | solution.py:106
  367.6 10.8 %gather_fusion.1 = f32[3072,96]{1,0:T(8,128)} fusion(f32[96,3072]{0,1:T(8,128)S(1)} %bitcast.98, s32[3072]{0:T(1024)S(1)} %get-tuple-element.8), kind=kCustom, calls=%fused_computation.1 | custom fusion | bytes 2371584 | tf_op jit(solution)/shard_map/gather | solution.py:113
  378.4 2.9 copy.39
  (36 shorter events, 6.3 us)
Async XLA Ops:
  7.2 246.6 %copy-start = (f32[1,384,384]{2,1,0:T(8,128)S(1)}, f32[1,384,384]{2,1,0:T(8,128)}, u32[]{:S(2)}) copy-start(f32[1,384,384]{2,1,0:T(8,128)} %param.12) | copy-start | bytes 1769476
  26.7 25.1 %copy-start.2 = (f32[96,3072]{1,0:T(8,128)S(1)}, f32[96,3072]{1,0:T(8,128)}, u32[]{:S(2)}) copy-start(f32[96,3072]{1,0:T(8,128)} %param.7) | copy-start | bytes 3538948
  40.3 21.3 %all-to-all-start = ((f32[1,64,48]{2,0,1:T(1,128)}), f32[1,64,48]{2,0,1:T(1,128)S(1)}, u32[]{:S(2)}, u32[]{:S(2)}) async-start(f32[1,64,48]{2,0,1:T(1,128)} %bitcast.4), calls=%async_computation | async-start | bytes 65536 | tf_op jit(solution)/shard_map/all_to_all | solution.py:44
  61.6 34.2 %all-to-all-start.1 = ((f32[96,64,48]{0,2,1:T(8,128)}), f32[96,64,48]{0,2,1:T(8,128)S(1)}, u32[]{:S(2)}, u32[]{:S(2)}) async-start(f32[96,64,48]{0,2,1:T(8,128)} %bitcast.7), calls=%async_computation.1 | async-start | bytes 3145728 | tf_op jit(solution)/shard_map/all_to_all | solution.py:37
  71.9 181.9 %all-reduce.4.cloned.1.call-start = ((), (), s32[]{:S(2)}) async-start(), calls=%async_computation.3 | async-start | bytes 589824 | tf_op jit(solution)/shard_map/psum | solution.py:63
  95.8 1.2 copy-start.1
  111.5 142.4 %copy-start.3 = (f32[96,384]{1,0:T(8,128)S(1)}, f32[96,384]{1,0:T(8,128)}, u32[]{:S(2)}) copy-start(f32[96,384]{1,0:T(8,128)} %param.11) | copy-start | bytes 442372
  115.4 162.4 %copy-start.4 = (bf16[2,1,384,384]{3,2,1,0:T(8,128)(2,1)S(1)}, bf16[2,1,384,384]{3,2,1,0:T(8,128)(2,1)}, u32[]{:S(2)}) copy-start(bf16[2,1,384,384]{3,2,1,0:T(8,128)(2,1)} %param.13) | copy-start | bytes 1769476
  115.5 162.4 %all-reduce.6.cloned.1.call-start = ((), (), s32[]{:S(2)}) async-start(), calls=%async_computation.4 | async-start | bytes 147456 | tf_op jit(solution)/shard_map/psum | solution.py:9
  255.9 50.3 %all-reduce.8.cloned.1.call-start = ((), (), s32[]{:S(2)}) async-start(), calls=%async_computation.5 | async-start | bytes 294912 | tf_op jit(solution)/shard_map/psum | solution.py:87
Sparse Core Ops, SparseCore 0:
  115.6 138.1 all-reduce.3
  256.8 21.0 all-reduce.5
  281.3 24.8 all-reduce.7
where the time goes:
time: 388 us
  waiting for transfers between devices  209 us (54%)
  local copies, waits for them, and re-layouts  58.6 us (15%)
  blocking collectives  37.2 us (10%)
  matrix products  27.3 us (7%)
  starting transfers between devices  22.1 us (6%)
  other arithmetic  20 us (5%)
  between operations  14 us (4%)
    psum x1, waiting for transfers between devices, shards(): totals = lax.psum(partial_sum, ('leaf', 'wide'))  138 us
    all_to_all x1, blocking collectives, shards(): lax.all_to_all(outgoing_back.reshape(side_count, wide_count, capacity), '...  35.3 us
    psum x1, waiting for transfers between devices, shards(): current = top_solved - lax.psum(term, 'leaf')  24.9 us
    all_to_all x1, waiting for transfers between devices, shards(): lax.all_to_all(outgoing.reshape(side_count, wide_count, capacity), 'wide'...  23.6 us
    psum x1, waiting for transfers between devices, spread(): return lax.psum(jnp.where(mine, shard, jnp.zeros_like(shard)), axis)  21.7 us
    another operation x3, other arithmetic  18.8 us
    scatter x1, local copies, waits for them, and re-layouts, shards(): places = jnp.full((wide_count * capacity,), float(row_count), jnp.float32...  11.8 us
    all_to_all x1, starting transfers between devices, shards(): lax.all_to_all(places.reshape(1, wide_count, capacity), 'wide', split_axi...  11.5 us
  transfers between devices with their start and end apart: 5, of which 4 were waited for; matrix products, arithmetic and copies ran while one was open for 3% of the time, Pallas kernels for 0%

commit v1 on v0

v1 whole, which is shorter than its diff:
```python
import functools

import jax
import jax.numpy as jnp
from jax import lax
from jax.experimental import pallas as pl
from jax.experimental.pallas import tpu as pltpu
from jax.sharding import PartitionSpec as P

MESH = pl.DeviceIdType.MESH
F32 = jnp.float32
BF16 = jnp.bfloat16
LANES = 128
TILE = 256


def dot(a, b):
    return jnp.dot(a, b, preferred_element_type=F32)


def dot_t(a, b):
    return lax.dot_general(a, b, (((1,), (1,)), ((), ())), preferred_element_type=F32)


def split(x):
    high = x.astype(BF16)
    return high, (x - high.astype(F32)).astype(BF16)


def iota(shape, dim):
    return lax.broadcasted_iota(jnp.int32, shape, dim)


def onehot(rows, values):
    shape = (rows, values.shape[1])
    match = iota(shape, 0).astype(F32) == jnp.broadcast_to(values, shape)
    return jnp.where(match, 1.0, 0.0).astype(BF16)


def invert_step(high, low, place, rows):
    first = onehot(rows, high).astype(F32)
    lane = iota((rows, LANES), 1).astype(F32)
    left = jnp.concatenate([first * place, first * lane], axis=0).astype(BF16)
    return dot_t(left, onehot(LANES, low))


def pick(data_ref, source, height, blocks):
    high = jnp.floor(source * (1.0 / TILE))
    chooser = onehot(TILE, source - TILE * high)
    result = None
    for block in range(blocks):
        part = dot(data_ref[:height, block * TILE : (block + 1) * TILE], chooser)
        if result is None:
            result = part
        else:
            result = jnp.where(jnp.broadcast_to(high == float(block), part.shape), part, result)
    return result


def row_pair(ref, pair):
    two = ref[pl.ds(2 * pair, 2), :]
    return jnp.concatenate([two[0:1], two[1:2]], axis=1)


def turned(x):
    height = x.shape[0]
    if height < LANES:
        x = jnp.concatenate([x, jnp.zeros((LANES - height, x.shape[1]), x.dtype)], axis=0)
    return x.T


def kernel(
    dims,
    index_ref,
    drop_ref,
    inverse_any,
    coupling_any,
    top_sides_ref,
    top_inverse_any,
    top_coupling_any,
    out_ref,
    top_out_ref,
    inverse_v,
    coupling_v,
    top_inv_f32,
    top_inv_high,
    top_inv_low,
    top_coup,
    inv_high,
    inv_low,
    slot_ref,
    source_ref,
    place_ref,
    data,
    received,
    super_n,
    low_solved,
    low_half,
    low_final,
    returned,
    send_buf,
    recv_buf,
    back_send,
    back_recv,
    partial,
    rs_send,
    rs_recv,
    pair_buf,
    ag_send,
    ag_recv,
    sol,
    load_sem,
    core_send,
    core_recv,
    local_sem,
    there_send,
    there_recv,
    back_send_sem,
    back_recv_sem,
    rs_send_sem,
    rs_recv_sem,
    ag_send_sem,
    ag_recv_sem,
):
    sides, rows, members, cap, nodes, width, owners = dims
    tiles = rows // LANES
    pairs = rows // TILE
    groups = 4
    chunks = members // groups
    group_rows = rows // groups
    group_pairs = pairs // groups
    group_tiles = tiles // groups
    top_cols = 2 * width
    col_tiles = top_cols // LANES
    own_rows = sides // owners
    me = lax.axis_index("wide")
    leaf = lax.axis_index("leaf")

    load_inverse = pltpu.make_async_copy(inverse_any, inverse_v, load_sem.at[0])
    load_coupling = pltpu.make_async_copy(coupling_any, coupling_v, load_sem.at[1])
    load_top = pltpu.make_async_copy(top_inverse_any.at[0], top_inv_f32.at[leaf], load_sem.at[2])
    load_tc = pltpu.make_async_copy(top_coupling_any.at[0, 0], top_coup.at[leaf], load_sem.at[3])
    load_inverse.start()
    load_coupling.start()
    load_top.start()
    load_tc.start()

    barrier = pltpu.get_barrier_semaphore()

    def greet(step, _):
        pl.semaphore_signal(
            barrier,
            inc=1,
            device_id={"wide": lax.rem(me + step, members)},
            device_id_type=MESH,
        )
        return 0

    lax.fori_loop(1, members, greet, 0)
    pl.semaphore_signal(barrier, inc=1, device_id={"leaf": 1 - leaf}, device_id_type=MESH)

    local = index_ref[...] - leaf * (members * rows)
    target = ((local.astype(F32) + 0.5) * (1.0 / rows)).astype(jnp.int32)
    position = (local - target * rows).astype(F32)
    relative = target - me - 1
    relative = jnp.where(relative < 0, relative + members, relative).astype(F32)
    place_high = jnp.floor(position * (1.0 / LANES))
    place_low = position - LANES * place_high
    below = (iota((LANES, LANES), 0) < iota((LANES, LANES), 1)).astype(F32)
    counter = jnp.concatenate([below, jnp.ones((LANES, LANES), F32)], axis=1).astype(BF16)
    carry = jnp.zeros((members, LANES), F32)
    inverse_sum = jnp.zeros((2 * tiles, LANES), F32)
    for tile in range(tiles):
        row = relative[tile : tile + 1]
        here = onehot(members, row)
        counts = dot(here, counter)
        rank = jnp.sum(here.astype(F32) * (counts[:, :LANES] + carry), axis=0, keepdims=True)
        carry = carry + counts[:, LANES:]
        slot = row * cap + rank
        slot_ref[tile : tile + 1, :] = slot
        slot_high = jnp.floor(slot * (1.0 / LANES))
        inverse_sum += invert_step(slot_high, slot - LANES * slot_high, float(tile), tiles)
        extra = iota((16, LANES), 0)
        extra = jnp.where(
            extra == 0, place_high[tile : tile + 1], jnp.where(extra == 1, place_low[tile : tile + 1], 0.0)
        )
        data[sides : sides + 16, tile * LANES : (tile + 1) * LANES] = extra.astype(BF16)
    source_ref[...] = LANES * inverse_sum[:tiles] + inverse_sum[tiles:]
    data[:sides, :] = drop_ref[...].astype(BF16)

    pl.semaphore_wait(barrier, members)

    load_top.wait()
    load_tc.wait()
    core_top = pltpu.make_async_remote_copy(
        src_ref=top_inv_f32.at[leaf],
        dst_ref=top_inv_f32.at[leaf],
        send_sem=core_send.at[0],
        recv_sem=core_recv.at[0],
        device_id={"leaf": 1 - leaf},
        device_id_type=MESH,
    )
    core_tc = pltpu.make_async_remote_copy(
        src_ref=top_coup.at[leaf],
        dst_ref=top_coup.at[leaf],
        send_sem=core_send.at[1],
        recv_sem=core_recv.at[1],
        device_id={"leaf": 1 - leaf},
        device_id_type=MESH,
    )
    core_top.start()
    core_tc.start()

    def there(chunk):
        return pltpu.make_async_remote_copy(
            src_ref=send_buf.at[chunk],
            dst_ref=recv_buf.at[chunk],
            send_sem=there_send,
            recv_sem=there_recv.at[chunk // chunks],
            device_id={"wide": lax.rem(me + 1 + chunk, members)},
            device_id_type=MESH,
        )

    def back(chunk):
        return pltpu.make_async_remote_copy(
            src_ref=back_send.at[chunk],
            dst_ref=back_recv.at[chunk],
            send_sem=back_send_sem,
            recv_sem=back_recv_sem.at[chunk // chunks],
            device_id={"wide": lax.rem(me - 1 - chunk + 2 * members, members)},
            device_id_type=MESH,
        )

    def start_group(copy, group):
        last = (group + 1) * chunks
        if group == groups - 1:
            last -= 1

        def begin(chunk, _):
            copy(chunk).start()
            return 0

        lax.fori_loop(group * chunks, last, begin, 0)

    def wait_group(buf, sem, group, dst=True):
        count = chunks - 1 if group == groups - 1 else chunks
        part = buf.at[pl.ds(group * chunks, count)]
        pltpu.make_async_remote_copy(
            src_ref=part,
            dst_ref=part,
            send_sem=there_send,
            recv_sem=sem.at[group],
            device_id={"wide": me},
            device_id_type=MESH,
        ).wait_recv()

    own_there = pltpu.make_async_copy(
        send_buf.at[members - 1], recv_buf.at[members - 1], local_sem.at[0]
    )
    own_back = pltpu.make_async_copy(
        back_send.at[members - 1], back_recv.at[members - 1], local_sem.at[1]
    )

    def store_chunks(buf, first, block):
        for piece in range(TILE // 16):
            at = first + piece
            buf[at // 3, pl.ds(pl.multiple_of((at % 3) * 16, 16), 16), :] = block[
                piece * 16 : (piece + 1) * 16
            ]

    for group in range(groups):
        for pair in range(group * group_pairs, (group + 1) * group_pairs):
            block = pick(data, row_pair(source_ref, pair), sides + 16, pairs)
            store_chunks(send_buf, pair * (TILE // 16), turned(block).astype(BF16))
        start_group(there, group)
    own_there.start()

    load_inverse.wait()

    def halves(node, _):
        high, low = split(inverse_v[node])
        inv_high[node] = high
        inv_low[node] = low
        return 0

    lax.fori_loop(0, nodes, halves, 0)
    core_top.wait()
    core_tc.wait()
    for half in range(2):
        high, low = split(top_inv_f32[half])
        top_inv_high[half] = high
        top_inv_low[half] = low

    inverse_sum = jnp.zeros((2 * tiles, LANES), F32)
    for group in range(groups):
        wait_group(recv_buf, there_recv, group)
        if group == groups - 1:
            own_there.wait()
        block = recv_buf[group * chunks : (group + 1) * chunks].reshape(group_rows, LANES)
        for tile in range(group_tiles):
            at = group * group_tiles + tile
            columns = block[tile * LANES : (tile + 1) * LANES].astype(F32).T
            received[:, at * LANES : (at + 1) * LANES] = columns[:sides].astype(BF16)
            high = columns[sides : sides + 1]
            low = columns[sides + 1 : sides + 2]
            place_ref[at : at + 1, :] = LANES * high + low
            inverse_sum += invert_step(high, low, float(at), tiles)
    source_ref[...] = LANES * inverse_sum[:tiles] + inverse_sum[tiles:]

    def unpack(pair, _):
        block = pick(received, row_pair(source_ref, pair), sides, pairs)
        super_n[:, pl.ds(pl.multiple_of(pair * TILE, TILE), TILE)] = block.astype(BF16)
        return 0

    lax.fori_loop(0, pairs, unpack, 0)

    def solve(node, _):
        span = pl.ds(pl.multiple_of(node * width, LANES), width)
        side = super_n[:, span]
        value = dot(side, inv_high[node]) + dot(side, inv_low[node])
        low_solved[:, span] = value
        low_half[:, span] = value.astype(BF16)
        return 0

    lax.fori_loop(0, nodes, solve, 0)

    load_coupling.wait()
    for part in range(top_cols // TILE):
        partial[:, part * TILE : (part + 1) * TILE] = dot(
            low_half[...], coupling_v[:, part * TILE : (part + 1) * TILE]
        )
    first = jnp.where(me == 0, 1.0, 0.0).astype(F32)
    own_columns = pl.ds(pl.multiple_of(leaf * width, LANES), width)
    partial[:, own_columns] = partial[:, own_columns] - top_sides_ref[...] * first

    def owner_chip(owner):
        return (owner * members) // owners

    for owner in range(owners):
        for col in range(col_tiles):
            rs_send[owner, col * own_rows : (col + 1) * own_rows, :] = partial[
                owner * own_rows : (owner + 1) * own_rows, col * LANES : (col + 1) * LANES
            ]

    def rs_copy(owner):
        chip = owner_chip(owner)
        return pltpu.make_async_remote_copy(
            src_ref=rs_send.at[owner],
            dst_ref=rs_recv.at[lax.rem(chip - me - 1 + members, members)],
            send_sem=rs_send_sem,
            recv_sem=rs_recv_sem,
            device_id={"wide": chip},
            device_id_type=MESH,
        )

    my_owner = (3 * me + 7) // 8
    is_owner = owner_chip(my_owner) == me

    def send_part(step, _):
        owner = lax.rem(my_owner + step, owners)

        @pl.when(owner_chip(owner) != me)
        def _():
            rs_copy(owner).start()

        return 0

    lax.fori_loop(0, owners, send_part, 0)

    def ag_copy(step):
        return pltpu.make_async_remote_copy(
            src_ref=ag_send,
            dst_ref=ag_recv.at[my_owner],
            send_sem=ag_send_sem,
            recv_sem=ag_recv_sem,
            device_id={"wide": lax.rem(me + step, members)},
            device_id_type=MESH,
        )

    def dummy(src, dst, send, recv):
        return pltpu.make_async_remote_copy(
            src_ref=src,
            dst_ref=dst,
            send_sem=send,
            recv_sem=recv,
            device_id={"wide": me},
            device_id_type=MESH,
        )

    @pl.when(is_owner)
    def _():
        mine = pltpu.make_async_copy(rs_send.at[my_owner], rs_recv.at[members - 1], local_sem.at[2])
        mine.start()
        mine.wait()
        arrived = rs_recv.at[pl.ds(0, members - 1)]
        dummy(arrived, arrived, rs_send_sem, rs_recv_sem).wait_recv()
        pair_buf[0] = jnp.sum(rs_recv[...], axis=0)
        swap = pltpu.make_async_remote_copy(
            src_ref=pair_buf.at[0],
            dst_ref=pair_buf.at[1],
            send_sem=core_send.at[2],
            recv_sem=core_recv.at[2],
            device_id={"leaf": 1 - leaf},
            device_id_type=MESH,
        )
        swap.start()
        swap.wait()
        total = pair_buf[0] + pair_buf[1]

        def columns_of(half):
            begin = half * (col_tiles // 2)
            return jnp.concatenate(
                [
                    total[(begin + col) * own_rows : (begin + col + 1) * own_rows]
                    for col in range(col_tiles // 2)
                ],
                axis=1,
            )

        def times(product, x, half):
            high, low = split(x)
            return (
                product(high, top_inv_high[half])
                + product(low, top_inv_high[half])
                + product(high, top_inv_low[half])
            )

        solved0 = times(dot, -columns_of(0), 0)
        solved1 = times(dot, -columns_of(1) - dot(solved0.astype(BF16), top_coup[1]), 1)
        answer1 = times(dot_t, solved1, 1)
        answer0 = times(dot_t, solved0 - dot_t(answer1.astype(BF16), top_coup[1]), 0)
        for col in range(col_tiles):
            half = (answer0, answer1)[col // (col_tiles // 2)]
            at = (col % (col_tiles // 2)) * LANES
            ag_send[col * own_rows : (col + 1) * own_rows, :] = half[:, at : at + LANES]
        keep = pltpu.make_async_copy(ag_send, ag_recv.at[my_owner], local_sem.at[3])
        keep.start()

        def tell(step, _):
            ag_copy(step).start()
            return 0

        lax.fori_loop(1, members, tell, 0)
        keep.wait()
        arrived = ag_recv.at[pl.ds(0, owners - 1)]
        dummy(arrived, arrived, ag_send_sem, ag_recv_sem).wait_recv()

    @pl.when(jnp.logical_not(is_owner))
    def _():
        dummy(ag_recv, ag_recv, ag_send_sem, ag_recv_sem).wait_recv()

    for owner in range(owners):
        for col in range(col_tiles):
            sol[owner * own_rows : (owner + 1) * own_rows, col * LANES : (col + 1) * LANES] = ag_recv[
                owner, col * own_rows : (col + 1) * own_rows, :
            ]
    top_out_ref[...] = sol[:, own_columns]
    sol_half = sol[...].astype(BF16)

    def finish(node, _):
        span = pl.ds(pl.multiple_of(node * width, LANES), width)
        term = dot_t(sol_half, coupling_v[pl.ds(pl.multiple_of(node * width, width), width), :])
        high, low = split(low_solved[:, span] - term)
        value = dot_t(high, inv_high[node]) + dot_t(low, inv_high[node]) + dot_t(high, inv_low[node])
        low_final[:, span] = value.astype(BF16)
        return 0

    lax.fori_loop(0, nodes, finish, 0)

    for group in range(groups):
        for pair in range(group * group_pairs, (group + 1) * group_pairs):
            block = pick(low_final, row_pair(place_ref, pair), sides, pairs)
            store_chunks(back_send, pair * (TILE // 16), turned(block).astype(BF16))
        start_group(back, group)
    own_back.start()

    for group in range(groups):
        wait_group(back_recv, back_recv_sem, group)
        if group == groups - 1:
            own_back.wait()
        block = back_recv[group * chunks : (group + 1) * chunks].reshape(group_rows, LANES)
        for tile in range(group_tiles):
            at = group * group_tiles + tile
            columns = block[tile * LANES : (tile + 1) * LANES].astype(F32).T
            returned[:, at * LANES : (at + 1) * LANES] = columns[:sides].astype(BF16)

    def last(pair, _):
        out_ref[:, pl.ds(pl.multiple_of(pair * TILE, TILE), TILE)] = pick(
            returned, row_pair(slot_ref, pair), sides, pairs
        )
        return 0

    lax.fori_loop(0, pairs, last, 0)

    sent = send_buf.at[pl.ds(0, members - 1)]
    dummy(sent, sent, there_send, there_send).wait_send()
    sent = back_send.at[pl.ds(0, members - 1)]
    dummy(sent, sent, back_send_sem, back_send_sem).wait_send()

    @pl.when(is_owner)
    def _():
        part = rs_send.at[pl.ds(0, owners - 1)]
        dummy(part, part, rs_send_sem, rs_send_sem).wait_send()
        part = rs_recv.at[pl.ds(0, members - 1)]
        dummy(part, part, ag_send_sem, ag_send_sem).wait_send()

    @pl.when(jnp.logical_not(is_owner))
    def _():
        dummy(rs_send, rs_send, rs_send_sem, rs_send_sem).wait_send()


def shards(drop_sides, super_index, low_inverse, coupling, top_sides, top_inverse, top_coupling):
    sides, rows = drop_sides.shape
    nodes, width, _ = low_inverse.shape
    members = lax.axis_size("wide")
    cap = rows // members
    owners = 24
    top_cols = coupling.shape[1]
    tiles = rows // LANES
    own = (sides // owners) * (top_cols // LANES)
    vmem = pl.BlockSpec(memory_space=pltpu.VMEM)
    anyspace = pl.BlockSpec(memory_space=pl.ANY)
    dma = pltpu.SemaphoreType.DMA
    dims = (sides, rows, members, cap, nodes, width, owners)
    return pl.pallas_call(
        functools.partial(kernel, dims),
        out_shape=(
            jax.ShapeDtypeStruct((sides, rows), F32),
            jax.ShapeDtypeStruct(top_sides.shape, F32),
        ),
        in_specs=[vmem, vmem, anyspace, anyspace, vmem, anyspace, anyspace],
        out_specs=(vmem, vmem),
        scratch_shapes=[
            pltpu.VMEM((nodes, width, width), F32),
            pltpu.VMEM((rows, top_cols), BF16),
            pltpu.VMEM((2, width, width), F32),
            pltpu.VMEM((2, width, width), BF16),
            pltpu.VMEM((2, width, width), BF16),
            pltpu.VMEM((2, width, width), BF16),
            pltpu.VMEM((nodes, width, width), BF16),
            pltpu.VMEM((nodes, width, width), BF16),
            pltpu.VMEM((tiles, LANES), F32),
            pltpu.VMEM((tiles, LANES), F32),
            pltpu.VMEM((tiles, LANES), F32),
            pltpu.VMEM((sides + 16, rows), BF16),
            pltpu.VMEM((sides, rows), BF16),
            pltpu.VMEM((sides, rows), BF16),
            pltpu.VMEM((sides, rows), F32),
            pltpu.VMEM((sides, rows), BF16),
            pltpu.VMEM((sides, rows), BF16),
            pltpu.VMEM((sides, rows), BF16),
            pltpu.VMEM((members, cap, LANES), BF16),
            pltpu.VMEM((members, cap, LANES), BF16),
            pltpu.VMEM((members, cap, LANES), BF16),
            pltpu.VMEM((members, cap, LANES), BF16),
            pltpu.VMEM((sides, top_cols), F32),
            pltpu.VMEM((owners, own, LANES), F32),
            pltpu.VMEM((members, own, LANES), F32),
            pltpu.VMEM((2, own, LANES), F32),
            pltpu.VMEM((own, LANES), F32),
            pltpu.VMEM((owners, own, LANES), F32),
            pltpu.VMEM((sides, top_cols), F32),
            dma((4,)),
            dma((3,)),
            dma((3,)),
            dma((4,)),
            dma,
            dma((4,)),
            dma,
            dma((4,)),
            dma,
            dma,
            dma,
            dma,
        ],
        compiler_params=pltpu.CompilerParams(
            collective_id=0, has_side_effects=True, vmem_limit_bytes=56 << 20
        ),
        name="substitution",
    )(
        super_index.reshape(tiles, LANES),
        drop_sides,
        low_inverse,
        coupling,
        top_sides,
        top_inverse,
        top_coupling,
    )


def solution(mesh):
    placed = (
        P(None, ("leaf", "wide")),
        P(("leaf", "wide")),
        P(("leaf", "wide"), None, None),
        P(("leaf", "wide"), None),
        P(None, "leaf"),
        P("leaf", None, None),
        P(None, "leaf", None, None),
    )
    return jax.shard_map(
        shards,
        mesh=mesh,
        in_specs=placed,
        out_specs=(P(None, ("leaf", "wide")), P(None, "leaf")),
        check_vma=False,
    )
```

time: 388 us -> 90.8 us (0.23)
  waiting for transfers between devices: 209 us -> 0 us
  Pallas kernels: 0 us -> 86.8 us
  local copies, waits for them, and re-layouts: 58.6 us -> 3.06 us
  blocking collectives: 37.2 us -> 0 us
  matrix products: 27.3 us -> 0 us
  starting transfers between devices: 22.1 us -> 0 us
  other arithmetic: 20 us -> 0 us
  between operations: 14 us -> 0.65 us
    psum x3 -> x0, waiting for transfers between devices: 185 us -> none  [the longest x1 138 us: shards(): totals = lax.psum(partial_sum, ('leaf', 'wide'))]
    pallas_call x0 -> x1, Pallas kernels: none -> 86.8 us  [shards(): pl.pallas_call(functools.partial(kernel, dims), out_shape=(jax.ShapeDtype...]
    all_to_all x1 -> x0, blocking collectives: 35.3 us -> none  [shards(): lax.all_to_all(outgoing_back.reshape(side_count, wide_count, capacity), '...]
    scatter x3 -> x0, local copies, waits for them, and re-layouts: 29.9 us -> none  [the longest x1 11.8 us: shards(): places = jnp.full((wide_count * capacity,), float(row_count), jnp.float32...]
    dot_general x10 -> x0, matrix products: 27.3 us -> none  [the longest x1 6.66 us: shards(): jnp.einsum('rsb,scb->rsc', (low_solved - low_term).reshape(side_count, no...]
    all_to_all x2 -> x0, waiting for transfers between devices: 23.6 us -> none  [the longest x1 23.6 us: shards(): lax.all_to_all(outgoing.reshape(side_count, wide_count, capacity), 'wide'...]
    all_to_all x2 -> x0, starting transfers between devices: 21.8 us -> none  [the longest x1 11.5 us: shards(): lax.all_to_all(places.reshape(1, wide_count, capacity), 'wide', split_axi...]
    gather x2 -> x0, local copies, waits for them, and re-layouts: 21.6 us -> none  [the longest x1 10.8 us: shards(): outgoing_back = low_solution[:, jnp.minimum(where_from, row_count - 1)]]
  transfers between devices with their start and end apart: 5 -> 0, of which waited for: 4 -> 0; matrix products, arithmetic and copies ran while one was open for 3% -> 0% of each run, Pallas kernels for 0% -> 0%
where the time goes in v1:
time: 90.8 us; the launch traced here: 90.6 us
  Pallas kernels  86.8 us (96%)
  local copies, waits for them, and re-layouts  3.06 us (3%)
    pallas_call x1, Pallas kernels, shards(): pl.pallas_call(functools.partial(kernel, dims), out_shape=(jax.ShapeDtype...  86.8 us
    unnamed x4, local copies, waits for them, and re-layouts  3.06 us

profile of v1, /device:TPU:0, one launch (start us, length us, event | category | flops | bytes accessed | tf_op | source)
XLA Modules:
  0.0 90.6 jit_solution(5873329938355003542)
XLA Ops:
  0.6 86.8 %substitution.1 = (f32[96,3072]{1,0:T(8,128)}, f32[96,384]{1,0:T(8,128)}) custom-call(s32[24,128]{1,0:T(8,128)} %bitcast.1, f32[96,3072]{1,0:T(8,128)} %drop_ref.1, f32[8,384,384]{2,1,0:T(8,128)} %inverse_any.1, bf16[3072,768]{1,0:T(8,128)(2,1)} %coupling_any.1, f32[96,384]{1,0:T(8,128)} %top_sides_ref.1, f32[1,384,384]{2,1,0:T(8,128)} %top_inverse_any.1, ...), custom_call_target="tpu_custom_call" | custom-call | tf_op jit(solution)/shard_map/substitution/pallas_call | solution.py:525
  87.5 0.0 copy-start
  87.5 2.4 %copy.11 = f32[96,3072]{1,0:T(8,128)} copy(f32[96,3072]{1,0:T(8,128)} %get-tuple-element.4) | data formatting | bytes 2359296
  89.9 0.0 copy-done
  89.9 0.7 copy.12
Async XLA Ops:
  87.5 2.4 %copy-start = (f32[96,384]{1,0:T(8,128)S(1)}, f32[96,384]{1,0:T(8,128)}, u32[]{:S(2)}) copy-start(f32[96,384]{1,0:T(8,128)} %get-tuple-element.5) | copy-start | bytes 442372

commit v2 on v1

--- a/solution.py
+++ b/solution.py
@@ -44,16 +44,15 @@
     return dot_t(left, onehot(LANES, low))
 
 
-def pick(data_ref, source, height, blocks):
+def pick(data_ref, source):
+    blocks, height, _ = data_ref.shape
     high = jnp.floor(source * (1.0 / TILE))
     chooser = onehot(TILE, source - TILE * high)
-    result = None
-    for block in range(blocks):
-        part = dot(data_ref[:height, block * TILE : (block + 1) * TILE], chooser)
-        if result is None:
-            result = part
-        else:
-            result = jnp.where(jnp.broadcast_to(high == float(block), part.shape), part, result)
+    parts = dot(data_ref[...].reshape(blocks * height, TILE), chooser)
+    result = parts[:height]
+    for block in range(1, blocks):
+        part = parts[block * height : (block + 1) * height]
+        result = jnp.where(jnp.broadcast_to(high == float(block), part.shape), part, result)
     return result
 
 
@@ -72,7 +71,7 @@
 def kernel(
     dims,
     index_ref,
-    drop_ref,
+    drop_any,
     inverse_any,
     coupling_any,
     top_sides_ref,
@@ -91,13 +90,16 @@
     slot_ref,
     source_ref,
     place_ref,
+    drop_v,
     data,
-    received,
+    turned_in,
+    place_wide,
     super_n,
     low_solved,
     low_half,
     low_final,
-    returned,
+    turned_back,
+    out_sum,
     send_buf,
     recv_buf,
     back_send,
@@ -136,15 +138,6 @@
     me = lax.axis_index("wide")
     leaf = lax.axis_index("leaf")
 
-    load_inverse = pltpu.make_async_copy(inverse_any, inverse_v, load_sem.at[0])
-    load_coupling = pltpu.make_async_copy(coupling_any, coupling_v, load_sem.at[1])
-    load_top = pltpu.make_async_copy(top_inverse_any.at[0], top_inv_f32.at[leaf], load_sem.at[2])
-    load_tc = pltpu.make_async_copy(top_coupling_any.at[0, 0], top_coup.at[leaf], load_sem.at[3])
-    load_inverse.start()
-    load_coupling.start()
-    load_top.start()
-    load_tc.start()
-
     barrier = pltpu.get_barrier_semaphore()
 
     def greet(step, _):
@@ -158,6 +151,17 @@
 
     lax.fori_loop(1, members, greet, 0)
     pl.semaphore_signal(barrier, inc=1, device_id={"leaf": 1 - leaf}, device_id_type=MESH)
+
+    load_drop = pltpu.make_async_copy(drop_any, drop_v, load_sem.at[4])
+    load_inverse = pltpu.make_async_copy(inverse_any, inverse_v, load_sem.at[0])
+    load_coupling = pltpu.make_async_copy(coupling_any, coupling_v, load_sem.at[1])
+    load_top = pltpu.make_async_copy(top_inverse_any.at[0], top_inv_f32.at[leaf], load_sem.at[2])
+    load_tc = pltpu.make_async_copy(top_coupling_any.at[0, 0], top_coup.at[leaf], load_sem.at[3])
+    load_drop.start()
+    load_inverse.start()
+    load_coupling.start()
+    load_top.start()
+    load_tc.start()
 
     local = index_ref[...] - leaf * (members * rows)
     target = ((local.astype(F32) + 0.5) * (1.0 / rows)).astype(jnp.int32)
@@ -170,6 +174,7 @@
     counter = jnp.concatenate([below, jnp.ones((LANES, LANES), F32)], axis=1).astype(BF16)
     carry = jnp.zeros((members, LANES), F32)
     inverse_sum = jnp.zeros((2 * tiles, LANES), F32)
+    extras = []
     for tile in range(tiles):
         row = relative[tile : tile + 1]
         here = onehot(members, row)
@@ -184,9 +189,21 @@
         extra = jnp.where(
             extra == 0, place_high[tile : tile + 1], jnp.where(extra == 1, place_low[tile : tile + 1], 0.0)
         )
-        data[sides : sides + 16, tile * LANES : (tile + 1) * LANES] = extra.astype(BF16)
+        extras.append(extra)
     source_ref[...] = LANES * inverse_sum[:tiles] + inverse_sum[tiles:]
-    data[:sides, :] = drop_ref[...].astype(BF16)
+
+    load_drop.wait()
+    for tile in range(tiles):
+        block, lanes = tile // 2, pl.ds((tile % 2) * LANES, LANES)
+        values = drop_v[:, tile * LANES : (tile + 1) * LANES]
+        most = jnp.maximum(jnp.max(jnp.abs(values), axis=0, keepdims=True), 2.0**-100)
+        power = jnp.ceil(jnp.log2(most) - 14.99)
+        code = jnp.floor(values * jnp.exp2(-power) + 0.5)
+        upper = jnp.floor(code * (1.0 / 256.0))
+        data[block, 0:sides, lanes] = upper.astype(BF16)
+        data[block, sides : 2 * sides, lanes] = (code - 256.0 * upper).astype(BF16)
+        extra = jnp.where(iota((16, LANES), 0) == 2, power, extras[tile])
+        data[block, 2 * sides : 2 * sides + 16, lanes] = extra.astype(BF16)
 
     pl.semaphore_wait(barrier, members)
 
@@ -270,8 +287,12 @@
 
     for group in range(groups):
         for pair in range(group * group_pairs, (group + 1) * group_pairs):
-            block = pick(data, row_pair(source_ref, pair), sides + 16, pairs)
-            store_chunks(send_buf, pair * (TILE // 16), turned(block).astype(BF16))
+            block = pick(data, row_pair(source_ref, pair))
+            code = jnp.concatenate(
+                [256.0 * block[:sides] + block[sides : 2 * sides], block[2 * sides :]], axis=0
+            )
+            code = turned(code).astype(jnp.int32).astype(jnp.int16)
+            store_chunks(send_buf, pair * (TILE // 16), code)
         start_group(there, group)
     own_there.start()
 
@@ -291,38 +312,49 @@
         top_inv_high[half] = high
         top_inv_low[half] = low
 
-    inverse_sum = jnp.zeros((2 * tiles, LANES), F32)
     for group in range(groups):
         wait_group(recv_buf, there_recv, group)
         if group == groups - 1:
             own_there.wait()
-        block = recv_buf[group * chunks : (group + 1) * chunks].reshape(group_rows, LANES)
         for tile in range(group_tiles):
             at = group * group_tiles + tile
-            columns = block[tile * LANES : (tile + 1) * LANES].astype(F32).T
-            received[:, at * LANES : (at + 1) * LANES] = columns[:sides].astype(BF16)
-            high = columns[sides : sides + 1]
-            low = columns[sides + 1 : sides + 2]
-            place_ref[at : at + 1, :] = LANES * high + low
-            inverse_sum += invert_step(high, low, float(at), tiles)
-    source_ref[...] = LANES * inverse_sum[:tiles] + inverse_sum[tiles:]
-
-    def unpack(pair, _):
-        block = pick(received, row_pair(source_ref, pair), sides, pairs)
-        super_n[:, pl.ds(pl.multiple_of(pair * TILE, TILE), TILE)] = block.astype(BF16)
-        return 0
-
-    lax.fori_loop(0, pairs, unpack, 0)
-
-    def solve(node, _):
-        span = pl.ds(pl.multiple_of(node * width, LANES), width)
-        side = super_n[:, span]
-        value = dot(side, inv_high[node]) + dot(side, inv_low[node])
+            first = group * chunks + (tile * LANES) // cap
+            last = group * chunks + ((tile + 1) * LANES - 1) // cap
+            skip = (tile * LANES) % cap
+            block = recv_buf[first : last + 1].astype(jnp.int32).astype(F32)
+            block = block.reshape((last + 1 - first) * cap, LANES)[skip : skip + LANES]
+            place = LANES * block[:, sides : sides + 1] + block[:, sides + 1 : sides + 2]
+            place_wide[tile * LANES : (tile + 1) * LANES, :] = jnp.broadcast_to(place, (LANES, LANES))
+            columns = block.T
+            place_ref[at : at + 1, :] = LANES * columns[sides : sides + 1] + columns[sides + 1 : sides + 2]
+            values = columns[:sides] * jnp.exp2(columns[sides + 2 : sides + 3])
+            high, low = split(values)
+            lanes = pl.ds(tile * LANES, LANES)
+            turned_in[:sides, lanes] = high
+            turned_in[sides:, lanes] = low
+
+        def arrive(pair, _):
+            lane = iota((group_rows, LANES), 1).astype(F32) + lax.convert_element_type(pair * TILE, F32)
+            there_is = place_wide[...]
+            chooser = jnp.concatenate(
+                [jnp.where(there_is == lane, 1.0, 0.0), jnp.where(there_is == lane + LANES, 1.0, 0.0)], axis=1
+            ).astype(BF16)
+            span = pl.ds(pl.multiple_of(pair * TILE, TILE), TILE)
+            value = dot(turned_in[...], chooser)
+            if group > 0:
+                value = value + super_n[:, span]
+            super_n[:, span] = value
+            return 0
+
+        lax.fori_loop(0, pairs, arrive, 0)
+
+    for node in range(nodes):
+        span = pl.ds(node * width, width)
+        side = super_n[:, span].astype(BF16)
+        value = dot(side, inv_high[node])
+        value = value[:sides] + value[sides:] + dot(side[:sides], inv_low[node])
         low_solved[:, span] = value
         low_half[:, span] = value.astype(BF16)
-        return 0
-
-    lax.fori_loop(0, nodes, solve, 0)
 
     load_coupling.wait()
     for part in range(top_cols // TILE):
@@ -457,19 +489,19 @@
     top_out_ref[...] = sol[:, own_columns]
     sol_half = sol[...].astype(BF16)
 
-    def finish(node, _):
-        span = pl.ds(pl.multiple_of(node * width, LANES), width)
-        term = dot_t(sol_half, coupling_v[pl.ds(pl.multiple_of(node * width, width), width), :])
+    for node in range(nodes):
+        span = pl.ds(node * width, width)
+        term = dot_t(sol_half, coupling_v[node * width : (node + 1) * width, :])
         high, low = split(low_solved[:, span] - term)
-        value = dot_t(high, inv_high[node]) + dot_t(low, inv_high[node]) + dot_t(high, inv_low[node])
-        low_final[:, span] = value.astype(BF16)
-        return 0
-
-    lax.fori_loop(0, nodes, finish, 0)
+        value = dot_t(jnp.concatenate([high, low], axis=0), inv_high[node])
+        value = (value[:sides] + value[sides:] + dot_t(high, inv_low[node])).astype(BF16)
+        for piece in range(width // LANES):
+            at = node * width + piece * LANES
+            low_final[at // TILE, :, pl.ds(at % TILE, LANES)] = value[:, piece * LANES : (piece + 1) * LANES]
 
     for group in range(groups):
         for pair in range(group * group_pairs, (group + 1) * group_pairs):
-            block = pick(low_final, row_pair(place_ref, pair), sides, pairs)
+            block = pick(low_final, row_pair(place_ref, pair))
             store_chunks(back_send, pair * (TILE // 16), turned(block).astype(BF16))
         start_group(back, group)
     own_back.start()
@@ -480,17 +512,22 @@
             own_back.wait()
         block = back_recv[group * chunks : (group + 1) * chunks].reshape(group_rows, LANES)
         for tile in range(group_tiles):
-            at = group * group_tiles + tile
             columns = block[tile * LANES : (tile + 1) * LANES].astype(F32).T
-            returned[:, at * LANES : (at + 1) * LANES] = columns[:sides].astype(BF16)
-
-    def last(pair, _):
-        out_ref[:, pl.ds(pl.multiple_of(pair * TILE, TILE), TILE)] = pick(
-            returned, row_pair(slot_ref, pair), sides, pairs
-        )
-        return 0
-
-    lax.fori_loop(0, pairs, last, 0)
+            turned_back[:, tile * LANES : (tile + 1) * LANES] = columns[:sides].astype(BF16)
+
+        def settle(pair, _):
+            chooser = onehot(group_rows, row_pair(slot_ref, pair) - float(group * group_rows))
+            span = pl.ds(pl.multiple_of(pair * TILE, TILE), TILE)
+            value = dot(turned_back[...], chooser)
+            if group > 0:
+                value = value + out_sum[:, span]
+            if group < groups - 1:
+                out_sum[:, span] = value
+            else:
+                out_ref[:, span] = value.astype(BF16)
+            return 0
+
+        lax.fori_loop(0, pairs, settle, 0)
 
     sent = send_buf.at[pl.ds(0, members - 1)]
     dummy(sent, sent, there_send, there_send).wait_send()
@@ -522,13 +559,13 @@
     anyspace = pl.BlockSpec(memory_space=pl.ANY)
     dma = pltpu.SemaphoreType.DMA
     dims = (sides, rows, members, cap, nodes, width, owners)
-    return pl.pallas_call(
+    low, top = pl.pallas_call(
         functools.partial(kernel, dims),
         out_shape=(
-            jax.ShapeDtypeStruct((sides, rows), F32),
+            jax.ShapeDtypeStruct((sides, rows), BF16),
             jax.ShapeDtypeStruct(top_sides.shape, F32),
         ),
-        in_specs=[vmem, vmem, anyspace, anyspace, vmem, anyspace, anyspace],
+        in_specs=[vmem, anyspace, anyspace, anyspace, vmem, anyspace, anyspace],
         out_specs=(vmem, vmem),
         scratch_shapes=[
             pltpu.VMEM((nodes, width, width), F32),
@@ -542,15 +579,18 @@
             pltpu.VMEM((tiles, LANES), F32),
             pltpu.VMEM((tiles, LANES), F32),
             pltpu.VMEM((tiles, LANES), F32),
-            pltpu.VMEM((sides + 16, rows), BF16),
-            pltpu.VMEM((sides, rows), BF16),
-            pltpu.VMEM((sides, rows), BF16),
+            pltpu.VMEM((sides, rows), F32),
+            pltpu.VMEM((rows // TILE, 2 * sides + 16, TILE), BF16),
+            pltpu.VMEM((2 * sides, rows // 4), BF16),
+            pltpu.VMEM((rows // 4, LANES), F32),
+            pltpu.VMEM((2 * sides, rows), F32),
             pltpu.VMEM((sides, rows), F32),
             pltpu.VMEM((sides, rows), BF16),
-            pltpu.VMEM((sides, rows), BF16),
-            pltpu.VMEM((sides, rows), BF16),
-            pltpu.VMEM((members, cap, LANES), BF16),
-            pltpu.VMEM((members, cap, LANES), BF16),
+            pltpu.VMEM((rows // TILE, sides, TILE), BF16),
+            pltpu.VMEM((sides, rows // 4), BF16),
+            pltpu.VMEM((sides, rows), F32),
+            pltpu.VMEM((members, cap, LANES), jnp.int16),
+            pltpu.VMEM((members, cap, LANES), jnp.int16),
             pltpu.VMEM((members, cap, LANES), BF16),
             pltpu.VMEM((members, cap, LANES), BF16),
             pltpu.VMEM((sides, top_cols), F32),
@@ -560,7 +600,7 @@
             pltpu.VMEM((own, LANES), F32),
             pltpu.VMEM((owners, own, LANES), F32),
             pltpu.VMEM((sides, top_cols), F32),
-            dma((4,)),
+            dma((5,)),
             dma((3,)),
             dma((3,)),
             dma((4,)),
@@ -586,6 +626,7 @@
         top_inverse,
         top_coupling,
     )
+    return low.astype(F32), top
 
 
 def solution(mesh):

time: 90.8 us -> 91.7 us (level)
  other arithmetic: 0 us -> 2.18 us
  local copies, waits for them, and re-layouts: 3.06 us -> 1.58 us
    convert_element_type x0 -> x1, other arithmetic: none -> 2.18 us  [shards(): return (low.astype(F32), top)]
    unnamed x4 -> x1, local copies, waits for them, and re-layouts: 3.06 us -> 1.58 us
where the time goes in v2:
time: 91.7 us; the launch traced here: 91.4 us
  Pallas kernels  87 us (95%)
  other arithmetic  2.18 us (2%)
  local copies, waits for them, and re-layouts  1.58 us (2%)
    pallas_call x1, Pallas kernels, shards(): pl.pallas_call(functools.partial(kernel, dims), out_shape=(jax.ShapeDtype...  87 us
    convert_element_type x1, other arithmetic, shards(): return (low.astype(F32), top)  2.18 us

profile of v2, /device:TPU:0, one launch (start us, length us, event | category | flops | bytes accessed | tf_op | source)
XLA Modules:
  0.0 91.4 jit_solution(2965182259028278527)
XLA Ops:
  0.6 87.0 %substitution.1 = (bf16[96,3072]{1,0:T(8,128)(2,1)}, f32[96,384]{1,0:T(8,128)}) custom-call(s32[24,128]{1,0:T(8,128)} %bitcast.1, f32[96,3072]{1,0:T(8,128)} %drop_any.1, f32[8,384,384]{2,1,0:T(8,128)} %inverse_any.1, bf16[3072,768]{1,0:T(8,128)(2,1)} %coupling_any.1, f32[96,384]{1,0:T(8,128)} %top_sides_ref.1, f32[1,384,384]{2,1,0:T(8,128)} %top_inverse_any.1, ...), custom_call_target="tpu_custom_call" | custom-call | tf_op jit(solution)/shard_map/substitution/pallas_call | solution.py:562
  87.6 2.2 %convert_element_type.3 = f32[96,3072]{1,0:T(8,128)} convert(bf16[96,3072]{1,0:T(8,128)(2,1)} %get-tuple-element.4) | non-fusion elementwise | flops 294912 | bytes 1769472 | tf_op jit(solution)/shard_map/convert_element_type | solution.py:629
  89.8 1.6 %copy.10 = f32[96,384]{1,0:T(8,128)} copy(f32[96,384]{1,0:T(8,128)} %get-tuple-element.9) | data formatting | bytes 294912

commit v3 on v2

--- a/solution.py
+++ b/solution.py
@@ -54,6 +54,29 @@
         part = parts[block * height : (block + 1) * height]
         result = jnp.where(jnp.broadcast_to(high == float(block), part.shape), part, result)
     return result
+
+
+def merge(data_ref, chooser, high, blocks, result):
+    count, height, _ = data_ref.shape
+    parts = dot(data_ref[...].reshape(count * height, TILE), chooser)
+    for at in range(count):
+        part = parts[at * height : (at + 1) * height]
+        if result is None:
+            result = part
+        else:
+            result = jnp.where(jnp.broadcast_to(high == float(blocks + at), part.shape), part, result)
+    return result
+
+
+def make_choosers(ref, chooser_ref, high_ref):
+    def one(pair, _):
+        source = row_pair(ref, pair)
+        high = jnp.floor(source * (1.0 / TILE))
+        chooser_ref[pair] = onehot(TILE, source - TILE * high)
+        high_ref[pl.ds(pair, 1), :] = high
+        return 0
+
+    lax.fori_loop(0, chooser_ref.shape[0], one, 0)
 
 
 def row_pair(ref, pair):
@@ -93,7 +116,14 @@
     drop_v,
     data,
     turned_in,
-    place_wide,
+    pos_send,
+    pos_recv,
+    choose_in,
+    choose_out,
+    choose_last,
+    high_in,
+    high_out,
+    high_last,
     super_n,
     low_solved,
     low_half,
@@ -117,6 +147,8 @@
     local_sem,
     there_send,
     there_recv,
+    pos_send_sem,
+    pos_recv_sem,
     back_send_sem,
     back_recv_sem,
     rs_send_sem,
@@ -175,6 +207,7 @@
     carry = jnp.zeros((members, LANES), F32)
     inverse_sum = jnp.zeros((2 * tiles, LANES), F32)
     extras = []
+    places = jnp.zeros((2 * members, LANES), F32)
     for tile in range(tiles):
         row = relative[tile : tile + 1]
         here = onehot(members, row)
@@ -183,6 +216,10 @@
         carry = carry + counts[:, LANES:]
         slot = row * cap + rank
         slot_ref[tile : tile + 1, :] = slot
+        both = jnp.concatenate(
+            [here * place_high[tile : tile + 1].astype(BF16), here * place_low[tile : tile + 1].astype(BF16)], axis=0
+        )
+        places = places + dot_t(both, onehot(LANES, rank))
         slot_high = jnp.floor(slot * (1.0 / LANES))
         inverse_sum += invert_step(slot_high, slot - LANES * slot_high, float(tile), tiles)
         extra = iota((16, LANES), 0)
@@ -191,6 +228,10 @@
         )
         extras.append(extra)
     source_ref[...] = LANES * inverse_sum[:tiles] + inverse_sum[tiles:]
+    places = jnp.where(iota((members, LANES), 1) < cap, LANES * places[:members] + places[members:], -1.0)
+    for member in range(members):
+        pos_send[member] = places[member : member + 1]
+    pos_recv[members - 1] = places[members - 1 : members]
 
     load_drop.wait()
     for tile in range(tiles):
@@ -206,6 +247,32 @@
         data[block, 2 * sides : 2 * sides + 16, lanes] = extra.astype(BF16)
 
     pl.semaphore_wait(barrier, members)
+
+    def dummy(src, dst, send, recv):
+        return pltpu.make_async_remote_copy(
+            src_ref=src,
+            dst_ref=dst,
+            send_sem=send,
+            recv_sem=recv,
+            device_id={"wide": me},
+            device_id_type=MESH,
+        )
+
+    def ahead(chunk):
+        return pltpu.make_async_remote_copy(
+            src_ref=pos_send.at[chunk],
+            dst_ref=pos_recv.at[chunk],
+            send_sem=pos_send_sem,
+            recv_sem=pos_recv_sem,
+            device_id={"wide": lax.rem(me + 1 + chunk, members)},
+            device_id_type=MESH,
+        )
+
+    def go_ahead(chunk, _):
+        ahead(chunk).start()
+        return 0
+
+    lax.fori_loop(0, members - 1, go_ahead, 0)
 
     load_top.wait()
     load_tc.wait()
@@ -312,6 +379,23 @@
         top_inv_high[half] = high
         top_inv_low[half] = low
 
+    arrived = pos_recv.at[pl.ds(0, members - 1)]
+    dummy(arrived, arrived, pos_send_sem, pos_recv_sem).wait_recv()
+    lane = iota((1, LANES), 1)
+    second = (lane >= LANES // 2).astype(F32)
+    offset = lane.astype(F32) - second * (LANES // 2)
+    inverse_sum = jnp.zeros((2 * tiles, LANES), F32)
+    for member in range(members // 2):
+        other = pltpu.roll(pos_recv[member + members // 2], LANES // 2, 1)
+        place = jnp.where(lane < LANES // 2, pos_recv[member], other)
+        high = jnp.floor(place * (1.0 / LANES))
+        first = onehot(tiles, high).astype(F32)
+        left = jnp.concatenate([first * (second * (members // 2) + float(member)), first * offset], axis=0)
+        inverse_sum += dot_t(left.astype(BF16), onehot(LANES, place - LANES * high))
+    source_ref[...] = cap * inverse_sum[:tiles] + inverse_sum[tiles:]
+    make_choosers(source_ref, choose_in, high_in)
+    make_choosers(slot_ref, choose_last, high_last)
+
     for group in range(groups):
         wait_group(recv_buf, there_recv, group)
         if group == groups - 1:
@@ -322,31 +406,20 @@
             last = group * chunks + ((tile + 1) * LANES - 1) // cap
             skip = (tile * LANES) % cap
             block = recv_buf[first : last + 1].astype(jnp.int32).astype(F32)
-            block = block.reshape((last + 1 - first) * cap, LANES)[skip : skip + LANES]
-            place = LANES * block[:, sides : sides + 1] + block[:, sides + 1 : sides + 2]
-            place_wide[tile * LANES : (tile + 1) * LANES, :] = jnp.broadcast_to(place, (LANES, LANES))
-            columns = block.T
+            columns = block.reshape((last + 1 - first) * cap, LANES)[skip : skip + LANES].T
             place_ref[at : at + 1, :] = LANES * columns[sides : sides + 1] + columns[sides + 1 : sides + 2]
             values = columns[:sides] * jnp.exp2(columns[sides + 2 : sides + 3])
             high, low = split(values)
-            lanes = pl.ds(tile * LANES, LANES)
-            turned_in[:sides, lanes] = high
-            turned_in[sides:, lanes] = low
-
-        def arrive(pair, _):
-            lane = iota((group_rows, LANES), 1).astype(F32) + lax.convert_element_type(pair * TILE, F32)
-            there_is = place_wide[...]
-            chooser = jnp.concatenate(
-                [jnp.where(there_is == lane, 1.0, 0.0), jnp.where(there_is == lane + LANES, 1.0, 0.0)], axis=1
-            ).astype(BF16)
-            span = pl.ds(pl.multiple_of(pair * TILE, TILE), TILE)
-            value = dot(turned_in[...], chooser)
-            if group > 0:
-                value = value + super_n[:, span]
-            super_n[:, span] = value
-            return 0
-
-        lax.fori_loop(0, pairs, arrive, 0)
+            lanes = pl.ds((tile % 2) * LANES, LANES)
+            turned_in[tile // 2, :sides, lanes] = high
+            turned_in[tile // 2, sides:, lanes] = low
+
+        for pair in range(pairs):
+            span = pl.ds(pair * TILE, TILE)
+            before = super_n[:, span] if group > 0 else None
+            super_n[:, span] = merge(
+                turned_in, choose_in[pair], high_in[pair : pair + 1], group * group_pairs, before
+            )
 
     for node in range(nodes):
         span = pl.ds(node * width, width)
@@ -399,6 +472,8 @@
 
     lax.fori_loop(0, owners, send_part, 0)
 
+    make_choosers(place_ref, choose_out, high_out)
+
     def ag_copy(step):
         return pltpu.make_async_remote_copy(
             src_ref=ag_send,
@@ -406,16 +481,6 @@
             send_sem=ag_send_sem,
             recv_sem=ag_recv_sem,
             device_id={"wide": lax.rem(me + step, members)},
-            device_id_type=MESH,
-        )
-
-    def dummy(src, dst, send, recv):
-        return pltpu.make_async_remote_copy(
-            src_ref=src,
-            dst_ref=dst,
-            send_sem=send,
-            recv_sem=recv,
-            device_id={"wide": me},
             device_id_type=MESH,
         )
 
@@ -501,7 +566,7 @@
 
     for group in range(groups):
         for pair in range(group * group_pairs, (group + 1) * group_pairs):
-            block = pick(low_final, row_pair(place_ref, pair))
+            block = merge(low_final, choose_out[pair], high_out[pair : pair + 1], 0, None)
             store_chunks(back_send, pair * (TILE // 16), turned(block).astype(BF16))
         start_group(back, group)
     own_back.start()
@@ -513,22 +578,21 @@
         block = back_recv[group * chunks : (group + 1) * chunks].reshape(group_rows, LANES)
         for tile in range(group_tiles):
             columns = block[tile * LANES : (tile + 1) * LANES].astype(F32).T
-            turned_back[:, tile * LANES : (tile + 1) * LANES] = columns[:sides].astype(BF16)
-
-        def settle(pair, _):
-            chooser = onehot(group_rows, row_pair(slot_ref, pair) - float(group * group_rows))
-            span = pl.ds(pl.multiple_of(pair * TILE, TILE), TILE)
-            value = dot(turned_back[...], chooser)
-            if group > 0:
-                value = value + out_sum[:, span]
+            turned_back[tile // 2, :, pl.ds((tile % 2) * LANES, LANES)] = columns[:sides].astype(BF16)
+
+        for pair in range(pairs):
+            span = pl.ds(pair * TILE, TILE)
+            before = out_sum[:, span] if group > 0 else None
+            value = merge(
+                turned_back, choose_last[pair], high_last[pair : pair + 1], group * group_pairs, before
+            )
             if group < groups - 1:
                 out_sum[:, span] = value
             else:
                 out_ref[:, span] = value.astype(BF16)
-            return 0
-
-        lax.fori_loop(0, pairs, settle, 0)
-
+
+    sent = pos_send.at[pl.ds(0, members - 1)]
+    dummy(sent, sent, pos_send_sem, pos_send_sem).wait_send()
     sent = send_buf.at[pl.ds(0, members - 1)]
     dummy(sent, sent, there_send, there_send).wait_send()
     sent = back_send.at[pl.ds(0, members - 1)]
@@ -581,13 +645,20 @@
             pltpu.VMEM((tiles, LANES), F32),
             pltpu.VMEM((sides, rows), F32),
             pltpu.VMEM((rows // TILE, 2 * sides + 16, TILE), BF16),
-            pltpu.VMEM((2 * sides, rows // 4), BF16),
-            pltpu.VMEM((rows // 4, LANES), F32),
+            pltpu.VMEM((rows // TILE // 4, 2 * sides, TILE), BF16),
+            pltpu.VMEM((members, 1, LANES), F32),
+            pltpu.VMEM((members, 1, LANES), F32),
+            pltpu.VMEM((rows // TILE, TILE, TILE), BF16),
+            pltpu.VMEM((rows // TILE, TILE, TILE), BF16),
+            pltpu.VMEM((rows // TILE, TILE, TILE), BF16),
+            pltpu.VMEM((rows // TILE, TILE), F32),
+            pltpu.VMEM((rows // TILE, TILE), F32),
+            pltpu.VMEM((rows // TILE, TILE), F32),
             pltpu.VMEM((2 * sides, rows), F32),
             pltpu.VMEM((sides, rows), F32),
             pltpu.VMEM((sides, rows), BF16),
             pltpu.VMEM((rows // TILE, sides, TILE), BF16),
-            pltpu.VMEM((sides, rows // 4), BF16),
+            pltpu.VMEM((rows // TILE // 4, sides, TILE), BF16),
             pltpu.VMEM((sides, rows), F32),
             pltpu.VMEM((members, cap, LANES), jnp.int16),
             pltpu.VMEM((members, cap, LANES), jnp.int16),
@@ -606,6 +677,8 @@
             dma((4,)),
             dma,
             dma((4,)),
+            dma,
+            dma,
             dma,
             dma((4,)),
             dma,

time: 91.7 us -> 83.7 us (0.913)
  Pallas kernels: 87 us -> 79.1 us
    pallas_call x1, Pallas kernels: 87 us -> 79.1 us  [shards(): pl.pallas_call(functools.partial(kernel, dims), out_shape=(jax.ShapeDtype...]
where the time goes in v3:
time: 83.7 us; the launch traced here: 83.5 us
  Pallas kernels  79.1 us (95%)
  other arithmetic  2.18 us (3%)
  local copies, waits for them, and re-layouts  1.58 us (2%)
    pallas_call x1, Pallas kernels, shards(): pl.pallas_call(functools.partial(kernel, dims), out_shape=(jax.ShapeDtype...  79.1 us
    convert_element_type x1, other arithmetic, shards(): return (low.astype(F32), top)  2.18 us

profile of v3, /device:TPU:0, one launch (start us, length us, event | category | flops | bytes accessed | tf_op | source)
XLA Modules:
  0.0 83.5 jit_solution(7412011751213557563)
XLA Ops:
  0.6 79.1 %substitution.1 = (bf16[96,3072]{1,0:T(8,128)(2,1)}, f32[96,384]{1,0:T(8,128)}) custom-call(s32[24,128]{1,0:T(8,128)} %bitcast.1, f32[96,3072]{1,0:T(8,128)} %drop_any.1, f32[8,384,384]{2,1,0:T(8,128)} %inverse_any.1, bf16[3072,768]{1,0:T(8,128)(2,1)} %coupling_any.1, f32[96,384]{1,0:T(8,128)} %top_sides_ref.1, f32[1,384,384]{2,1,0:T(8,128)} %top_inverse_any.1, ...), custom_call_target="tpu_custom_call" | custom-call | tf_op jit(solution)/shard_map/substitution/pallas_call | solution.py:626
  79.8 2.2 %convert_element_type.3 = f32[96,3072]{1,0:T(8,128)} convert(bf16[96,3072]{1,0:T(8,128)(2,1)} %get-tuple-element.4) | non-fusion elementwise | flops 294912 | bytes 1769472 | tf_op jit(solution)/shard_map/convert_element_type | solution.py:702
  82.0 1.6 %copy.10 = f32[96,384]{1,0:T(8,128)} copy(f32[96,384]{1,0:T(8,128)} %get-tuple-element.9) | data formatting | bytes 294912

commit v4 on v3

--- a/solution.py
+++ b/solution.py
@@ -135,12 +135,14 @@
     back_send,
     back_recv,
     partial,
+    half_send,
+    half_recv,
     rs_send,
     rs_recv,
     pair_buf,
     ag_send,
     ag_recv,
-    sol,
+    sol_half,
     load_sem,
     core_send,
     core_recv,
@@ -164,8 +166,6 @@
     group_rows = rows // groups
     group_pairs = pairs // groups
     group_tiles = tiles // groups
-    top_cols = 2 * width
-    col_tiles = top_cols // LANES
     own_rows = sides // owners
     me = lax.axis_index("wide")
     leaf = lax.axis_index("leaf")
@@ -430,22 +430,35 @@
         low_half[:, span] = value.astype(BF16)
 
     load_coupling.wait()
-    for part in range(top_cols // TILE):
-        partial[:, part * TILE : (part + 1) * TILE] = dot(
-            low_half[...], coupling_v[:, part * TILE : (part + 1) * TILE]
-        )
+
+    def half_sum(half):
+        return dot(low_half[...], coupling_v[:, pl.ds(pl.multiple_of(half * width, LANES), width)])
+
+    half_send[...] = half_sum(1 - leaf)
+    core_half = pltpu.make_async_remote_copy(
+        src_ref=half_send,
+        dst_ref=half_recv,
+        send_sem=core_send.at[3],
+        recv_sem=core_recv.at[3],
+        device_id={"leaf": 1 - leaf},
+        device_id_type=MESH,
+    )
+    core_half.start()
     first = jnp.where(me == 0, 1.0, 0.0).astype(F32)
-    own_columns = pl.ds(pl.multiple_of(leaf * width, LANES), width)
-    partial[:, own_columns] = partial[:, own_columns] - top_sides_ref[...] * first
+    partial[...] = half_sum(leaf) - top_sides_ref[...] * first
+    core_half.wait()
+    partial[...] = partial[...] + half_recv[...]
+    for owner in range(owners):
+        rs_send[owner] = partial[owner * own_rows : (owner + 1) * own_rows, :]
 
     def owner_chip(owner):
-        return (owner * members) // owners
-
-    for owner in range(owners):
-        for col in range(col_tiles):
-            rs_send[owner, col * own_rows : (col + 1) * own_rows, :] = partial[
-                owner * own_rows : (owner + 1) * own_rows, col * LANES : (col + 1) * LANES
-            ]
+        line = owner // 3
+        return 4 * line + lax.rem(owner - 3 * line + line + line // 4, 4)
+
+    my_line = me // 4
+    my_turn = lax.rem(me - 4 * my_line + 8 * members - my_line - my_line // 4, 4)
+    is_owner = my_turn < 3
+    my_owner = 3 * my_line + jnp.minimum(my_turn, 2)
 
     def rs_copy(owner):
         chip = owner_chip(owner)
@@ -458,9 +471,6 @@
             device_id_type=MESH,
         )
 
-    my_owner = (3 * me + 7) // 8
-    is_owner = owner_chip(my_owner) == me
-
     def send_part(step, _):
         owner = lax.rem(my_owner + step, owners)
 
@@ -471,7 +481,6 @@
         return 0
 
     lax.fori_loop(0, owners, send_part, 0)
-
     make_choosers(place_ref, choose_out, high_out)
 
     def ag_copy(step):
@@ -486,15 +495,13 @@
 
     @pl.when(is_owner)
     def _():
-        mine = pltpu.make_async_copy(rs_send.at[my_owner], rs_recv.at[members - 1], local_sem.at[2])
-        mine.start()
-        mine.wait()
+        rs_recv[members - 1] = rs_send[my_owner]
         arrived = rs_recv.at[pl.ds(0, members - 1)]
         dummy(arrived, arrived, rs_send_sem, rs_recv_sem).wait_recv()
-        pair_buf[0] = jnp.sum(rs_recv[...], axis=0)
+        pair_buf[leaf] = jnp.sum(rs_recv[...], axis=0)
         swap = pltpu.make_async_remote_copy(
-            src_ref=pair_buf.at[0],
-            dst_ref=pair_buf.at[1],
+            src_ref=pair_buf.at[leaf],
+            dst_ref=pair_buf.at[leaf],
             send_sem=core_send.at[2],
             recv_sem=core_recv.at[2],
             device_id={"leaf": 1 - leaf},
@@ -502,17 +509,6 @@
         )
         swap.start()
         swap.wait()
-        total = pair_buf[0] + pair_buf[1]
-
-        def columns_of(half):
-            begin = half * (col_tiles // 2)
-            return jnp.concatenate(
-                [
-                    total[(begin + col) * own_rows : (begin + col + 1) * own_rows]
-                    for col in range(col_tiles // 2)
-                ],
-                axis=1,
-            )
 
         def times(product, x, half):
             high, low = split(x)
@@ -522,23 +518,18 @@
                 + product(high, top_inv_low[half])
             )
 
-        solved0 = times(dot, -columns_of(0), 0)
-        solved1 = times(dot, -columns_of(1) - dot(solved0.astype(BF16), top_coup[1]), 1)
+        solved0 = times(dot, -pair_buf[0], 0)
+        solved1 = times(dot, -pair_buf[1] - dot(solved0.astype(BF16), top_coup[1]), 1)
         answer1 = times(dot_t, solved1, 1)
         answer0 = times(dot_t, solved0 - dot_t(answer1.astype(BF16), top_coup[1]), 0)
-        for col in range(col_tiles):
-            half = (answer0, answer1)[col // (col_tiles // 2)]
-            at = (col % (col_tiles // 2)) * LANES
-            ag_send[col * own_rows : (col + 1) * own_rows, :] = half[:, at : at + LANES]
-        keep = pltpu.make_async_copy(ag_send, ag_recv.at[my_owner], local_sem.at[3])
-        keep.start()
+        ag_send[...] = jnp.where(leaf == 0, answer0, answer1)
+        ag_recv[my_owner] = ag_send[...]
 
         def tell(step, _):
             ag_copy(step).start()
             return 0
 
         lax.fori_loop(1, members, tell, 0)
-        keep.wait()
         arrived = ag_recv.at[pl.ds(0, owners - 1)]
         dummy(arrived, arrived, ag_send_sem, ag_recv_sem).wait_recv()
 
@@ -547,16 +538,23 @@
         dummy(ag_recv, ag_recv, ag_send_sem, ag_recv_sem).wait_recv()
 
     for owner in range(owners):
-        for col in range(col_tiles):
-            sol[owner * own_rows : (owner + 1) * own_rows, col * LANES : (col + 1) * LANES] = ag_recv[
-                owner, col * own_rows : (col + 1) * own_rows, :
-            ]
-    top_out_ref[...] = sol[:, own_columns]
-    sol_half = sol[...].astype(BF16)
+        top_out_ref[owner * own_rows : (owner + 1) * own_rows, :] = ag_recv[owner]
+    sol_half[leaf] = top_out_ref[...].astype(BF16)
+    core_sol = pltpu.make_async_remote_copy(
+        src_ref=sol_half.at[leaf],
+        dst_ref=sol_half.at[leaf],
+        send_sem=core_send.at[4],
+        recv_sem=core_recv.at[4],
+        device_id={"leaf": 1 - leaf},
+        device_id_type=MESH,
+    )
+    core_sol.start()
+    core_sol.wait()
 
     for node in range(nodes):
         span = pl.ds(node * width, width)
-        term = dot_t(sol_half, coupling_v[node * width : (node + 1) * width, :])
+        rows_here = slice(node * width, (node + 1) * width)
+        term = dot_t(sol_half[0], coupling_v[rows_here, :width]) + dot_t(sol_half[1], coupling_v[rows_here, width:])
         high, low = split(low_solved[:, span] - term)
         value = dot_t(jnp.concatenate([high, low], axis=0), inv_high[node])
         value = (value[:sides] + value[sides:] + dot_t(high, inv_low[node])).astype(BF16)
@@ -610,15 +608,23 @@
         dummy(rs_send, rs_send, rs_send_sem, rs_send_sem).wait_send()
 
 
+def widen(low_ref, top_ref, out_ref, top_out_ref):
+    out_ref[...] = low_ref[...].astype(F32)
+
+    @pl.when(pl.program_id(0) == 0)
+    def _():
+        top_out_ref[...] = top_ref[...]
+
+
 def shards(drop_sides, super_index, low_inverse, coupling, top_sides, top_inverse, top_coupling):
     sides, rows = drop_sides.shape
     nodes, width, _ = low_inverse.shape
     members = lax.axis_size("wide")
     cap = rows // members
-    owners = 24
+    owners = 48
     top_cols = coupling.shape[1]
     tiles = rows // LANES
-    own = (sides // owners) * (top_cols // LANES)
+    own = sides // owners
     vmem = pl.BlockSpec(memory_space=pltpu.VMEM)
     anyspace = pl.BlockSpec(memory_space=pl.ANY)
     dma = pltpu.SemaphoreType.DMA
@@ -664,16 +670,18 @@
             pltpu.VMEM((members, cap, LANES), jnp.int16),
             pltpu.VMEM((members, cap, LANES), BF16),
             pltpu.VMEM((members, cap, LANES), BF16),
-            pltpu.VMEM((sides, top_cols), F32),
-            pltpu.VMEM((owners, own, LANES), F32),
-            pltpu.VMEM((members, own, LANES), F32),
-            pltpu.VMEM((2, own, LANES), F32),
-            pltpu.VMEM((own, LANES), F32),
-            pltpu.VMEM((owners, own, LANES), F32),
-            pltpu.VMEM((sides, top_cols), F32),
+            pltpu.VMEM((sides, width), F32),
+            pltpu.VMEM((sides, width), F32),
+            pltpu.VMEM((sides, width), F32),
+            pltpu.VMEM((owners, own, width), F32),
+            pltpu.VMEM((members, own, width), F32),
+            pltpu.VMEM((2, own, width), F32),
+            pltpu.VMEM((own, width), F32),
+            pltpu.VMEM((owners, own, width), F32),
+            pltpu.VMEM((2, sides, width), BF16),
             dma((5,)),
-            dma((3,)),
-            dma((3,)),
+            dma((5,)),
+            dma((5,)),
             dma((4,)),
             dma,
             dma((4,)),
@@ -699,7 +707,20 @@
         top_inverse,
         top_coupling,
     )
-    return low.astype(F32), top
+    return pl.pallas_call(
+        widen,
+        grid=(4,),
+        out_shape=(jax.ShapeDtypeStruct((sides, rows), F32), jax.ShapeDtypeStruct(top_sides.shape, F32)),
+        in_specs=[
+            pl.BlockSpec((sides, rows // 4), lambda at: (0, at)),
+            pl.BlockSpec(top_sides.shape, lambda at: (0, 0)),
+        ],
+        out_specs=(
+            pl.BlockSpec((sides, rows // 4), lambda at: (0, at)),
+            pl.BlockSpec(top_sides.shape, lambda at: (0, 0)),
+        ),
+        name="widen",
+    )(low, top)
 
 
 def solution(mesh):

time: 83.7 us -> 76.9 us (0.919)
  Pallas kernels: 79.1 us -> 76.1 us
  other arithmetic: 2.18 us -> 0 us
  local copies, waits for them, and re-layouts: 1.58 us -> 0 us
    pallas_call x1, Pallas kernels: 79.1 us -> 72.6 us  [shards(): pl.pallas_call(functools.partial(kernel, dims), out_shape=(jax.ShapeDtype...]
    pallas_call x0 -> x1, Pallas kernels: none -> 3.45 us  [shards(): pl.pallas_call(widen, grid=(4,), out_shape=(jax.ShapeDtypeStruct((sides,...]
    convert_element_type x1 -> x0, other arithmetic: 2.18 us -> none  [shards(): return (low.astype(F32), top)]
    unnamed x1 -> x0, local copies, waits for them, and re-layouts: 1.58 us -> none
where the time goes in v4:
time: 76.9 us; the launch traced here: 76.7 us
  Pallas kernels  76.1 us (99%)
    pallas_call x1, Pallas kernels, shards(): pl.pallas_call(functools.partial(kernel, dims), out_shape=(jax.ShapeDtype...  72.6 us
    pallas_call x1, Pallas kernels, shards(): pl.pallas_call(widen, grid=(4,), out_shape=(jax.ShapeDtypeStruct((sides,...  3.45 us

profile of v4, /device:TPU:0, one launch (start us, length us, event | category | flops | bytes accessed | tf_op | source)
XLA Modules:
  0.0 76.7 jit_solution(12769501229812137415)
XLA Ops:
  0.6 72.6 %substitution.1 = (bf16[96,3072]{1,0:T(8,128)(2,1)}, f32[96,384]{1,0:T(8,128)}) custom-call(s32[24,128]{1,0:T(8,128)} %bitcast.1, f32[96,3072]{1,0:T(8,128)} %drop_any.1, f32[8,384,384]{2,1,0:T(8,128)} %inverse_any.1, bf16[3072,768]{1,0:T(8,128)(2,1)} %coupling_any.1, f32[96,384]{1,0:T(8,128)} %top_sides_ref.1, f32[1,384,384]{2,1,0:T(8,128)} %top_inverse_any.1, ...), custom_call_target="tpu_custom_call" | custom-call | tf_op jit(solution)/shard_map/substitution/pallas_call | solution.py:632
  73.2 3.4 %widen.1 = (f32[96,3072]{1,0:T(8,128)}, f32[96,384]{1,0:T(8,128)}) custom-call(bf16[96,3072]{1,0:T(8,128)(2,1)} %get-tuple-element.4.low_ref, f32[96,384]{1,0:T(8,128)} %get-tuple-element.5.top_ref), custom_call_target="tpu_custom_call" | custom-call | tf_op jit(solution)/shard_map/widen/pallas_call | solution.py:710

commit v5 on v4

--- a/solution.py
+++ b/solution.py
@@ -1,4 +1,5 @@
 import functools
+import random
 
 import jax
 import jax.numpy as jnp
@@ -12,6 +13,15 @@
 BF16 = jnp.bfloat16
 LANES = 128
 TILE = 256
+
+
+def order_of_partners():
+    steps = [(z, y, x) for z in range(4) for y in range(4) for x in range(4)][1:]
+    random.Random(2).shuffle(steps)
+    return sorted(steps, key=lambda step: -sum((0, 1, 2, 1)[one] for one in step)) + [(0, 0, 0)]
+
+
+ORDER = order_of_partners()
 
 
 def dot(a, b):
@@ -93,15 +103,24 @@
 
 def kernel(
     dims,
-    index_ref,
+    index_any,
     drop_any,
     inverse_any,
     coupling_any,
-    top_sides_ref,
+    top_sides_any,
     top_inverse_any,
     top_coupling_any,
-    out_ref,
-    top_out_ref,
+    out_any,
+    top_out_any,
+    index_v,
+    top_sides_v,
+    out_v,
+    top_out_v,
+    here_ref,
+    left_slot,
+    right_slot,
+    left_place,
+    right_place,
     inverse_v,
     coupling_v,
     top_inv_f32,
@@ -157,6 +176,7 @@
     rs_recv_sem,
     ag_send_sem,
     ag_recv_sem,
+    out_sem,
 ):
     sides, rows, members, cap, nodes, width, owners = dims
     tiles = rows // LANES
@@ -169,6 +189,19 @@
     own_rows = sides // owners
     me = lax.axis_index("wide")
     leaf = lax.axis_index("leaf")
+    my_z, my_y, my_x = me // 16, lax.rem(me // 4, 4), lax.rem(me, 4)
+    z_at = [16 * lax.rem(my_z + step, 4) for step in range(4)]
+    y_at = [4 * lax.rem(my_y + step, 4) for step in range(4)]
+    x_at = [lax.rem(my_x + step, 4) for step in range(4)]
+
+    def partner(chunk):
+        dz, dy, dx = ORDER[chunk]
+        return z_at[dz] + y_at[dy] + x_at[dx]
+
+    def origin(chunk):
+        dz, dy, dx = ORDER[chunk]
+        return z_at[(4 - dz) % 4] + y_at[(4 - dy) % 4] + x_at[(4 - dx) % 4]
+
 
     barrier = pltpu.get_barrier_semaphore()
 
@@ -184,50 +217,72 @@
     lax.fori_loop(1, members, greet, 0)
     pl.semaphore_signal(barrier, inc=1, device_id={"leaf": 1 - leaf}, device_id_type=MESH)
 
+    load_index = pltpu.make_async_copy(index_any, index_v, load_sem.at[5])
+    load_sides = pltpu.make_async_copy(top_sides_any, top_sides_v, load_sem.at[6])
     load_drop = pltpu.make_async_copy(drop_any, drop_v, load_sem.at[4])
     load_inverse = pltpu.make_async_copy(inverse_any, inverse_v, load_sem.at[0])
     load_coupling = pltpu.make_async_copy(coupling_any, coupling_v, load_sem.at[1])
     load_top = pltpu.make_async_copy(top_inverse_any.at[0], top_inv_f32.at[leaf], load_sem.at[2])
     load_tc = pltpu.make_async_copy(top_coupling_any.at[0, 0], top_coup.at[leaf], load_sem.at[3])
+    load_index.start()
     load_drop.start()
     load_inverse.start()
     load_coupling.start()
     load_top.start()
     load_tc.start()
-
-    local = index_ref[...] - leaf * (members * rows)
+    load_sides.start()
+
+    order = jnp.zeros((members, LANES), F32)
+    chunk_of = iota((members, LANES), 0)
+    for chunk, (dz, dy, dx) in enumerate(ORDER):
+        order = jnp.where(chunk_of == chunk, float(16 * dz + 4 * dy + dx), order)
+    begin = (cap * chunk_of).astype(F32)
+    below = (iota((LANES, LANES), 0) < iota((LANES, LANES), 1)).astype(F32)
+    counter = jnp.concatenate([below, jnp.ones((LANES, LANES), F32)], axis=1).astype(BF16)
+    load_index.wait()
+    local = index_v[...] - leaf * (members * rows)
     target = ((local.astype(F32) + 0.5) * (1.0 / rows)).astype(jnp.int32)
     position = (local - target * rows).astype(F32)
-    relative = target - me - 1
-    relative = jnp.where(relative < 0, relative + members, relative).astype(F32)
+    step_of = (
+        16 * (((target >> 4) - my_z) & 3) + 4 * (((target >> 2) - my_y) & 3) + ((target - my_x) & 3)
+    ).astype(F32)
     place_high = jnp.floor(position * (1.0 / LANES))
     place_low = position - LANES * place_high
-    below = (iota((LANES, LANES), 0) < iota((LANES, LANES), 1)).astype(F32)
-    counter = jnp.concatenate([below, jnp.ones((LANES, LANES), F32)], axis=1).astype(BF16)
+
+    def here_of(tile):
+        return jnp.where(order == step_of[tile : tile + 1], 1.0, 0.0)
+
+    for tile in range(tiles):
+        here_ref[tile * members : (tile + 1) * members, :] = here_of(tile).astype(BF16)
+    counts = dot(here_ref[...], counter)
     carry = jnp.zeros((members, LANES), F32)
-    inverse_sum = jnp.zeros((2 * tiles, LANES), F32)
+    lane = iota((tiles, LANES), 1).astype(F32)
     extras = []
-    places = jnp.zeros((2 * members, LANES), F32)
     for tile in range(tiles):
-        row = relative[tile : tile + 1]
-        here = onehot(members, row)
-        counts = dot(here, counter)
-        rank = jnp.sum(here.astype(F32) * (counts[:, :LANES] + carry), axis=0, keepdims=True)
-        carry = carry + counts[:, LANES:]
-        slot = row * cap + rank
+        here = here_of(tile)
+        count = counts[tile * members : (tile + 1) * members]
+        rank = jnp.sum(here * (count[:, :LANES] + carry), axis=0, keepdims=True)
+        slot = rank + jnp.sum(here * begin, axis=0, keepdims=True)
+        carry = carry + count[:, LANES:]
         slot_ref[tile : tile + 1, :] = slot
-        both = jnp.concatenate(
-            [here * place_high[tile : tile + 1].astype(BF16), here * place_low[tile : tile + 1].astype(BF16)], axis=0
+        slot_high = jnp.floor(slot * (1.0 / LANES))
+        span = pl.ds(tile * LANES, LANES)
+        first = onehot(tiles, slot_high).astype(F32)
+        left_slot[:, span] = jnp.concatenate([first * float(tile), first * lane], axis=0).astype(BF16)
+        right_slot[:, span] = onehot(LANES, slot - LANES * slot_high)
+        left_place[:, span] = jnp.concatenate(
+            [here * place_high[tile : tile + 1], here * place_low[tile : tile + 1]], axis=0
+        ).astype(BF16)
+        right_place[:, span] = onehot(LANES, rank)
+        extra = iota((16, LANES), 0)
+        extras.append(
+            jnp.where(
+                extra == 0, place_high[tile : tile + 1], jnp.where(extra == 1, place_low[tile : tile + 1], 0.0)
+            )
         )
-        places = places + dot_t(both, onehot(LANES, rank))
-        slot_high = jnp.floor(slot * (1.0 / LANES))
-        inverse_sum += invert_step(slot_high, slot - LANES * slot_high, float(tile), tiles)
-        extra = iota((16, LANES), 0)
-        extra = jnp.where(
-            extra == 0, place_high[tile : tile + 1], jnp.where(extra == 1, place_low[tile : tile + 1], 0.0)
-        )
-        extras.append(extra)
+    inverse_sum = dot_t(left_slot[...], right_slot[...])
     source_ref[...] = LANES * inverse_sum[:tiles] + inverse_sum[tiles:]
+    places = dot_t(left_place[...], right_place[...])
     places = jnp.where(iota((members, LANES), 1) < cap, LANES * places[:members] + places[members:], -1.0)
     for member in range(members):
         pos_send[member] = places[member : member + 1]
@@ -264,15 +319,12 @@
             dst_ref=pos_recv.at[chunk],
             send_sem=pos_send_sem,
             recv_sem=pos_recv_sem,
-            device_id={"wide": lax.rem(me + 1 + chunk, members)},
+            device_id={"wide": partner(chunk)},
             device_id_type=MESH,
         )
 
-    def go_ahead(chunk, _):
+    for chunk in range(members - 1):
         ahead(chunk).start()
-        return 0
-
-    lax.fori_loop(0, members - 1, go_ahead, 0)
 
     load_top.wait()
     load_tc.wait()
@@ -301,7 +353,7 @@
             dst_ref=recv_buf.at[chunk],
             send_sem=there_send,
             recv_sem=there_recv.at[chunk // chunks],
-            device_id={"wide": lax.rem(me + 1 + chunk, members)},
+            device_id={"wide": partner(chunk)},
             device_id_type=MESH,
         )
 
@@ -311,7 +363,7 @@
             dst_ref=back_recv.at[chunk],
             send_sem=back_send_sem,
             recv_sem=back_recv_sem.at[chunk // chunks],
-            device_id={"wide": lax.rem(me - 1 - chunk + 2 * members, members)},
+            device_id={"wide": origin(chunk)},
             device_id_type=MESH,
         )
 
@@ -320,11 +372,8 @@
         if group == groups - 1:
             last -= 1
 
-        def begin(chunk, _):
+        for chunk in range(group * chunks, last):
             copy(chunk).start()
-            return 0
-
-        lax.fori_loop(group * chunks, last, begin, 0)
 
     def wait_group(buf, sem, group, dst=True):
         count = chunks - 1 if group == groups - 1 else chunks
@@ -445,51 +494,47 @@
     )
     core_half.start()
     first = jnp.where(me == 0, 1.0, 0.0).astype(F32)
-    partial[...] = half_sum(leaf) - top_sides_ref[...] * first
+    load_sides.wait()
+    partial[...] = half_sum(leaf) - top_sides_v[...] * first
     core_half.wait()
     partial[...] = partial[...] + half_recv[...]
     for owner in range(owners):
         rs_send[owner] = partial[owner * own_rows : (owner + 1) * own_rows, :]
 
-    def owner_chip(owner):
-        line = owner // 3
-        return 4 * line + lax.rem(owner - 3 * line + line + line // 4, 4)
-
-    my_line = me // 4
-    my_turn = lax.rem(me - 4 * my_line + 8 * members - my_line - my_line // 4, 4)
+    def turn_of(chip):
+        line = chip // 4
+        return lax.rem(chip - 4 * line + 8 * members - line - line // 4, 4)
+
+    my_turn = turn_of(me)
     is_owner = my_turn < 3
-    my_owner = 3 * my_line + jnp.minimum(my_turn, 2)
-
-    def rs_copy(owner):
-        chip = owner_chip(owner)
-        return pltpu.make_async_remote_copy(
-            src_ref=rs_send.at[owner],
-            dst_ref=rs_recv.at[lax.rem(chip - me - 1 + members, members)],
-            send_sem=rs_send_sem,
-            recv_sem=rs_recv_sem,
-            device_id={"wide": chip},
-            device_id_type=MESH,
-        )
-
-    def send_part(step, _):
-        owner = lax.rem(my_owner + step, owners)
-
-        @pl.when(owner_chip(owner) != me)
+    my_owner = 3 * (me // 4) + jnp.minimum(my_turn, 2)
+
+    def send_part(chunk):
+        chip = partner(chunk)
+        turn = turn_of(chip)
+
+        @pl.when(turn < 3)
         def _():
-            rs_copy(owner).start()
-
-        return 0
-
-    lax.fori_loop(0, owners, send_part, 0)
+            pltpu.make_async_remote_copy(
+                src_ref=rs_send.at[3 * (chip // 4) + jnp.minimum(turn, 2)],
+                dst_ref=rs_recv.at[chunk],
+                send_sem=rs_send_sem,
+                recv_sem=rs_recv_sem,
+                device_id={"wide": chip},
+                device_id_type=MESH,
+            ).start()
+
+    for chunk in range(members - 1):
+        send_part(chunk)
     make_choosers(place_ref, choose_out, high_out)
 
-    def ag_copy(step):
+    def ag_copy(chunk):
         return pltpu.make_async_remote_copy(
             src_ref=ag_send,
             dst_ref=ag_recv.at[my_owner],
             send_sem=ag_send_sem,
             recv_sem=ag_recv_sem,
-            device_id={"wide": lax.rem(me + step, members)},
+            device_id={"wide": partner(chunk)},
             device_id_type=MESH,
         )
 
@@ -525,11 +570,8 @@
         ag_send[...] = jnp.where(leaf == 0, answer0, answer1)
         ag_recv[my_owner] = ag_send[...]
 
-        def tell(step, _):
-            ag_copy(step).start()
-            return 0
-
-        lax.fori_loop(1, members, tell, 0)
+        for chunk in range(members - 1):
+            ag_copy(chunk).start()
         arrived = ag_recv.at[pl.ds(0, owners - 1)]
         dummy(arrived, arrived, ag_send_sem, ag_recv_sem).wait_recv()
 
@@ -538,8 +580,8 @@
         dummy(ag_recv, ag_recv, ag_send_sem, ag_recv_sem).wait_recv()
 
     for owner in range(owners):
-        top_out_ref[owner * own_rows : (owner + 1) * own_rows, :] = ag_recv[owner]
-    sol_half[leaf] = top_out_ref[...].astype(BF16)
+        top_out_v[owner * own_rows : (owner + 1) * own_rows, :] = ag_recv[owner]
+    sol_half[leaf] = top_out_v[...].astype(BF16)
     core_sol = pltpu.make_async_remote_copy(
         src_ref=sol_half.at[leaf],
         dst_ref=sol_half.at[leaf],
@@ -549,6 +591,8 @@
         device_id_type=MESH,
     )
     core_sol.start()
+    store_top = pltpu.make_async_copy(top_out_v, top_out_any, local_sem.at[2])
+    store_top.start()
     core_sol.wait()
 
     for node in range(nodes):
@@ -569,6 +613,10 @@
         start_group(back, group)
     own_back.start()
 
+    def store_out(part):
+        span = pl.ds(part * 3 * TILE, 3 * TILE)
+        return pltpu.make_async_copy(out_v.at[:, span], out_any.at[:, span], out_sem.at[part])
+
     for group in range(groups):
         wait_group(back_recv, back_recv_sem, group)
         if group == groups - 1:
@@ -587,8 +635,13 @@
             if group < groups - 1:
                 out_sum[:, span] = value
             else:
-                out_ref[:, span] = value.astype(BF16)
-
+                out_v[:, span] = value.astype(BF16)
+                if pair % 3 == 2:
+                    store_out(pair // 3).start()
+
+    store_top.wait()
+    for part in range(pairs // 3):
+        store_out(part).wait()
     sent = pos_send.at[pl.ds(0, members - 1)]
     dummy(sent, sent, pos_send_sem, pos_send_sem).wait_send()
     sent = send_buf.at[pl.ds(0, members - 1)]
@@ -625,7 +678,6 @@
     top_cols = coupling.shape[1]
     tiles = rows // LANES
     own = sides // owners
-    vmem = pl.BlockSpec(memory_space=pltpu.VMEM)
     anyspace = pl.BlockSpec(memory_space=pl.ANY)
     dma = pltpu.SemaphoreType.DMA
     dims = (sides, rows, members, cap, nodes, width, owners)
@@ -635,9 +687,18 @@
             jax.ShapeDtypeStruct((sides, rows), BF16),
             jax.ShapeDtypeStruct(top_sides.shape, F32),
         ),
-        in_specs=[vmem, anyspace, anyspace, anyspace, vmem, anyspace, anyspace],
-        out_specs=(vmem, vmem),
+        in_specs=[anyspace] * 7,
+        out_specs=(anyspace, anyspace),
         scratch_shapes=[
+            pltpu.VMEM((tiles, LANES), jnp.int32),
+            pltpu.VMEM((sides, width), F32),
+            pltpu.VMEM((sides, rows), BF16),
+            pltpu.VMEM((sides, width), F32),
+            pltpu.VMEM((tiles * members, LANES), BF16),
+            pltpu.VMEM((2 * tiles, rows), BF16),
+            pltpu.VMEM((LANES, rows), BF16),
+            pltpu.VMEM((2 * members, rows), BF16),
+            pltpu.VMEM((LANES, rows), BF16),
             pltpu.VMEM((nodes, width, width), F32),
             pltpu.VMEM((rows, top_cols), BF16),
             pltpu.VMEM((2, width, width), F32),
@@ -679,7 +740,7 @@
             pltpu.VMEM((own, width), F32),
             pltpu.VMEM((owners, own, width), F32),
             pltpu.VMEM((2, sides, width), BF16),
-            dma((5,)),
+            dma((7,)),
             dma((5,)),
             dma((5,)),
             dma((4,)),
@@ -693,6 +754,7 @@
             dma,
             dma,
             dma,
+            dma((4,)),
         ],
         compiler_params=pltpu.CompilerParams(
             collective_id=0, has_side_effects=True, vmem_limit_bytes=56 << 20
@@ -709,14 +771,14 @@
     )
     return pl.pallas_call(
         widen,
-        grid=(4,),
+        grid=(2,),
         out_shape=(jax.ShapeDtypeStruct((sides, rows), F32), jax.ShapeDtypeStruct(top_sides.shape, F32)),
         in_specs=[
-            pl.BlockSpec((sides, rows // 4), lambda at: (0, at)),
+            pl.BlockSpec((sides, rows // 2), lambda at: (0, at)),
             pl.BlockSpec(top_sides.shape, lambda at: (0, 0)),
         ],
         out_specs=(
-            pl.BlockSpec((sides, rows // 4), lambda at: (0, at)),
+            pl.BlockSpec((sides, rows // 2), lambda at: (0, at)),
             pl.BlockSpec(top_sides.shape, lambda at: (0, 0)),
         ),
         name="widen",

time: 76.9 us -> 69.5 us (0.904)
  Pallas kernels: 76.1 us -> 67.9 us
    pallas_call x1, Pallas kernels: 72.6 us -> 65.8 us  [shards(): pl.pallas_call(functools.partial(kernel, dims), out_shape=(jax.ShapeDtype...]
    pallas_call x1, Pallas kernels: 3.45 us -> 2.12 us  [shards(): pl.pallas_call(widen, grid=(2,), out_shape=(jax.ShapeDtypeStruct((sides,...]
where the time goes in v5:
time: 69.5 us; the launch traced here: 68.5 us
  Pallas kernels  67.9 us (98%)
    pallas_call x1, Pallas kernels, shards(): pl.pallas_call(functools.partial(kernel, dims), out_shape=(jax.ShapeDtype...  65.8 us
    pallas_call x1, Pallas kernels, shards(): pl.pallas_call(widen, grid=(2,), out_shape=(jax.ShapeDtypeStruct((sides,...  2.12 us

profile of v5, /device:TPU:0, one launch (start us, length us, event | category | flops | bytes accessed | tf_op | source)
XLA Modules:
  0.0 68.5 jit_solution(17765178796232589666)
XLA Ops:
  0.6 65.8 %substitution.1 = (bf16[96,3072]{1,0:T(8,128)(2,1)}, f32[96,384]{1,0:T(8,128)}) custom-call(s32[24,128]{1,0:T(8,128)} %bitcast.1, f32[96,3072]{1,0:T(8,128)} %drop_any.1, f32[8,384,384]{2,1,0:T(8,128)} %inverse_any.1, bf16[3072,768]{1,0:T(8,128)(2,1)} %coupling_any.1, f32[96,384]{1,0:T(8,128)} %top_sides_any.1, f32[1,384,384]{2,1,0:T(8,128)} %top_inverse_any.1, ...), custom_call_target="tpu_custom_call" | custom-call | tf_op jit(solution)/shard_map/substitution/pallas_call | solution.py:684
  66.4 2.1 %widen.1 = (f32[96,3072]{1,0:T(8,128)}, f32[96,384]{1,0:T(8,128)}) custom-call(bf16[96,3072]{1,0:T(8,128)(2,1)} %get-tuple-element.4.low_ref, f32[96,384]{1,0:T(8,128)} %get-tuple-element.5.top_ref), custom_call_target="tpu_custom_call" | custom-call | tf_op jit(solution)/shard_map/widen/pallas_call | solution.py:772

commit v6 on v5

--- a/solution.py
+++ b/solution.py
@@ -145,6 +145,8 @@
     high_last,
     super_n,
     low_solved,
+    base,
+    weighed,
     low_half,
     low_final,
     turned_back,
@@ -268,7 +270,9 @@
         slot_high = jnp.floor(slot * (1.0 / LANES))
         span = pl.ds(tile * LANES, LANES)
         first = onehot(tiles, slot_high).astype(F32)
-        left_slot[:, span] = jnp.concatenate([first * float(tile), first * lane], axis=0).astype(BF16)
+        left_slot[:, span] = jnp.concatenate(
+            [first * float(tile), first * lane, jnp.zeros((LANES - 2 * tiles, LANES), F32)], axis=0
+        ).astype(BF16)
         right_slot[:, span] = onehot(LANES, slot - LANES * slot_high)
         left_place[:, span] = jnp.concatenate(
             [here * place_high[tile : tile + 1], here * place_low[tile : tile + 1]], axis=0
@@ -280,8 +284,8 @@
                 extra == 0, place_high[tile : tile + 1], jnp.where(extra == 1, place_low[tile : tile + 1], 0.0)
             )
         )
-    inverse_sum = dot_t(left_slot[...], right_slot[...])
-    source_ref[...] = LANES * inverse_sum[:tiles] + inverse_sum[tiles:]
+    inverse_sum = dot_t(right_slot[...], left_slot[...]).T
+    source_ref[...] = LANES * inverse_sum[:tiles] + inverse_sum[tiles : 2 * tiles]
     places = dot_t(left_place[...], right_place[...])
     places = jnp.where(iota((members, LANES), 1) < cap, LANES * places[:members] + places[members:], -1.0)
     for member in range(members):
@@ -300,6 +304,22 @@
         data[block, sides : 2 * sides, lanes] = (code - 256.0 * upper).astype(BF16)
         extra = jnp.where(iota((16, LANES), 0) == 2, power, extras[tile])
         data[block, 2 * sides : 2 * sides + 16, lanes] = extra.astype(BF16)
+
+    def store_chunks(buf, first, block):
+        for piece in range(TILE // 16):
+            at = first + piece
+            buf[at // 3, pl.ds(pl.multiple_of((at % 3) * 16, 16), 16), :] = block[
+                piece * 16 : (piece + 1) * 16
+            ]
+
+    for group in range(groups):
+        for pair in range(group * group_pairs, (group + 1) * group_pairs):
+            block = pick(data, row_pair(source_ref, pair))
+            code = jnp.concatenate(
+                [256.0 * block[:sides] + block[sides : 2 * sides], block[2 * sides :]], axis=0
+            )
+            code = turned(code).astype(jnp.int32).astype(jnp.int16)
+            store_chunks(send_buf, pair * (TILE // 16), code)
 
     pl.semaphore_wait(barrier, members)
 
@@ -394,21 +414,7 @@
         back_send.at[members - 1], back_recv.at[members - 1], local_sem.at[1]
     )
 
-    def store_chunks(buf, first, block):
-        for piece in range(TILE // 16):
-            at = first + piece
-            buf[at // 3, pl.ds(pl.multiple_of((at % 3) * 16, 16), 16), :] = block[
-                piece * 16 : (piece + 1) * 16
-            ]
-
     for group in range(groups):
-        for pair in range(group * group_pairs, (group + 1) * group_pairs):
-            block = pick(data, row_pair(source_ref, pair))
-            code = jnp.concatenate(
-                [256.0 * block[:sides] + block[sides : 2 * sides], block[2 * sides :]], axis=0
-            )
-            code = turned(code).astype(jnp.int32).astype(jnp.int16)
-            store_chunks(send_buf, pair * (TILE // 16), code)
         start_group(there, group)
     own_there.start()
 
@@ -528,6 +534,20 @@
         send_part(chunk)
     make_choosers(place_ref, choose_out, high_out)
 
+    for node in range(nodes):
+        span = pl.ds(node * width, width)
+        high, low = split(low_solved[:, span])
+        value = dot_t(jnp.concatenate([high, low], axis=0), inv_high[node])
+        base[:, span] = value[:sides] + value[sides:] + dot_t(high, inv_low[node])
+
+    def weigh(node, _):
+        span = pl.ds(pl.multiple_of(node * width, width), width)
+        block = coupling_v[span, :]
+        weighed[span, :] = (dot(inv_high[node], block) + dot(inv_low[node], block)).astype(BF16)
+        return 0
+
+    lax.fori_loop(0, nodes // 2, weigh, 0)
+
     def ag_copy(chunk):
         return pltpu.make_async_remote_copy(
             src_ref=ag_send,
@@ -557,11 +577,8 @@
 
         def times(product, x, half):
             high, low = split(x)
-            return (
-                product(high, top_inv_high[half])
-                + product(low, top_inv_high[half])
-                + product(high, top_inv_low[half])
-            )
+            both = product(jnp.concatenate([high, low], axis=0), top_inv_high[half])
+            return both[:own_rows] + both[own_rows:] + product(high, top_inv_low[half])
 
         solved0 = times(dot, -pair_buf[0], 0)
         solved1 = times(dot, -pair_buf[1] - dot(solved0.astype(BF16), top_coup[1]), 1)
@@ -572,6 +589,11 @@
 
         for chunk in range(members - 1):
             ag_copy(chunk).start()
+
+    lax.fori_loop(nodes // 2, nodes, weigh, 0)
+
+    @pl.when(is_owner)
+    def _():
         arrived = ag_recv.at[pl.ds(0, owners - 1)]
         dummy(arrived, arrived, ag_send_sem, ag_recv_sem).wait_recv()
 
@@ -598,10 +620,8 @@
     for node in range(nodes):
         span = pl.ds(node * width, width)
         rows_here = slice(node * width, (node + 1) * width)
-        term = dot_t(sol_half[0], coupling_v[rows_here, :width]) + dot_t(sol_half[1], coupling_v[rows_here, width:])
-        high, low = split(low_solved[:, span] - term)
-        value = dot_t(jnp.concatenate([high, low], axis=0), inv_high[node])
-        value = (value[:sides] + value[sides:] + dot_t(high, inv_low[node])).astype(BF16)
+        term = dot_t(sol_half[0], weighed[rows_here, :width]) + dot_t(sol_half[1], weighed[rows_here, width:])
+        value = (base[:, span] - term).astype(BF16)
         for piece in range(width // LANES):
             at = node * width + piece * LANES
             low_final[at // TILE, :, pl.ds(at % TILE, LANES)] = value[:, piece * LANES : (piece + 1) * LANES]
@@ -695,7 +715,7 @@
             pltpu.VMEM((sides, rows), BF16),
             pltpu.VMEM((sides, width), F32),
             pltpu.VMEM((tiles * members, LANES), BF16),
-            pltpu.VMEM((2 * tiles, rows), BF16),
+            pltpu.VMEM((LANES, rows), BF16),
             pltpu.VMEM((LANES, rows), BF16),
             pltpu.VMEM((2 * members, rows), BF16),
             pltpu.VMEM((LANES, rows), BF16),
@@ -723,6 +743,8 @@
             pltpu.VMEM((rows // TILE, TILE), F32),
             pltpu.VMEM((2 * sides, rows), F32),
             pltpu.VMEM((sides, rows), F32),
+            pltpu.VMEM((sides, rows), F32),
+            pltpu.VMEM((rows, top_cols), BF16),
             pltpu.VMEM((sides, rows), BF16),
             pltpu.VMEM((rows // TILE, sides, TILE), BF16),
             pltpu.VMEM((rows // TILE // 4, sides, TILE), BF16),

time: 69.5 us -> 68.9 us (level)
  no operation moved by 1% of the time
where the time goes in v6:
time: 68.9 us; the launch traced here: 68.2 us
  Pallas kernels  67.6 us (98%)
    pallas_call x1, Pallas kernels, shards(): pl.pallas_call(functools.partial(kernel, dims), out_shape=(jax.ShapeDtype...  65.5 us
    pallas_call x1, Pallas kernels, shards(): pl.pallas_call(widen, grid=(2,), out_shape=(jax.ShapeDtypeStruct((sides,...  2.12 us

profile of v6, /device:TPU:0, one launch (start us, length us, event | category | flops | bytes accessed | tf_op | source)
XLA Modules:
  0.0 68.2 jit_solution(2698233759808543792)
XLA Ops:
  0.6 65.5 %substitution.1 = (bf16[96,3072]{1,0:T(8,128)(2,1)}, f32[96,384]{1,0:T(8,128)}) custom-call(s32[24,128]{1,0:T(8,128)} %bitcast.1, f32[96,3072]{1,0:T(8,128)} %drop_any.1, f32[8,384,384]{2,1,0:T(8,128)} %inverse_any.1, bf16[3072,768]{1,0:T(8,128)(2,1)} %coupling_any.1, f32[96,384]{1,0:T(8,128)} %top_sides_any.1, f32[1,384,384]{2,1,0:T(8,128)} %top_inverse_any.1, ...), custom_call_target="tpu_custom_call" | custom-call | tf_op jit(solution)/shard_map/substitution/pallas_call | solution.py:704
  66.1 2.1 %widen.1 = (f32[96,3072]{1,0:T(8,128)}, f32[96,384]{1,0:T(8,128)}) custom-call(bf16[96,3072]{1,0:T(8,128)(2,1)} %get-tuple-element.4.low_ref, f32[96,384]{1,0:T(8,128)} %get-tuple-element.5.top_ref), custom_call_target="tpu_custom_call" | custom-call | tf_op jit(solution)/shard_map/widen/pallas_call | solution.py:794

commit v7 on v6

--- a/solution.py
+++ b/solution.py
@@ -312,7 +312,7 @@
                 piece * 16 : (piece + 1) * 16
             ]
 
-    for group in range(groups):
+    def pack(group):
         for pair in range(group * group_pairs, (group + 1) * group_pairs):
             block = pick(data, row_pair(source_ref, pair))
             code = jnp.concatenate(
@@ -320,6 +320,8 @@
             )
             code = turned(code).astype(jnp.int32).astype(jnp.int16)
             store_chunks(send_buf, pair * (TILE // 16), code)
+
+    pack(0)
 
     pl.semaphore_wait(barrier, members)
 
@@ -414,7 +416,9 @@
         back_send.at[members - 1], back_recv.at[members - 1], local_sem.at[1]
     )
 
-    for group in range(groups):
+    start_group(there, 0)
+    for group in range(1, groups):
+        pack(group)
         start_group(there, group)
     own_there.start()
 
@@ -534,12 +538,6 @@
         send_part(chunk)
     make_choosers(place_ref, choose_out, high_out)
 
-    for node in range(nodes):
-        span = pl.ds(node * width, width)
-        high, low = split(low_solved[:, span])
-        value = dot_t(jnp.concatenate([high, low], axis=0), inv_high[node])
-        base[:, span] = value[:sides] + value[sides:] + dot_t(high, inv_low[node])
-
     def weigh(node, _):
         span = pl.ds(pl.multiple_of(node * width, width), width)
         block = coupling_v[span, :]
@@ -589,6 +587,12 @@
 
         for chunk in range(members - 1):
             ag_copy(chunk).start()
+
+    for node in range(nodes):
+        span = pl.ds(node * width, width)
+        high, low = split(low_solved[:, span])
+        value = dot_t(jnp.concatenate([high, low], axis=0), inv_high[node])
+        base[:, span] = value[:sides] + value[sides:] + dot_t(high, inv_low[node])
 
     lax.fori_loop(nodes // 2, nodes, weigh, 0)
 

time: 68.9 us -> 65.5 us (0.951)
  Pallas kernels: 67.6 us -> 63.9 us
    pallas_call x1, Pallas kernels: 65.5 us -> 61.8 us  [shards(): pl.pallas_call(functools.partial(kernel, dims), out_shape=(jax.ShapeDtype...]
where the time goes in v7:
time: 65.5 us; the launch traced here: 64.5 us
  Pallas kernels  63.9 us (98%)
    pallas_call x1, Pallas kernels, shards(): pl.pallas_call(functools.partial(kernel, dims), out_shape=(jax.ShapeDtype...  61.8 us
    pallas_call x1, Pallas kernels, shards(): pl.pallas_call(widen, grid=(2,), out_shape=(jax.ShapeDtypeStruct((sides,...  2.12 us

profile of v7, /device:TPU:0, one launch (start us, length us, event | category | flops | bytes accessed | tf_op | source)
XLA Modules:
  0.0 64.5 jit_solution(14531017089597734522)
XLA Ops:
  0.6 61.8 %substitution.1 = (bf16[96,3072]{1,0:T(8,128)(2,1)}, f32[96,384]{1,0:T(8,128)}) custom-call(s32[24,128]{1,0:T(8,128)} %bitcast.1, f32[96,3072]{1,0:T(8,128)} %drop_any.1, f32[8,384,384]{2,1,0:T(8,128)} %inverse_any.1, bf16[3072,768]{1,0:T(8,128)(2,1)} %coupling_any.1, f32[96,384]{1,0:T(8,128)} %top_sides_any.1, f32[1,384,384]{2,1,0:T(8,128)} %top_inverse_any.1, ...), custom_call_target="tpu_custom_call" | custom-call | tf_op jit(solution)/shard_map/substitution/pallas_call | solution.py:708
  62.4 2.1 %widen.1 = (f32[96,3072]{1,0:T(8,128)}, f32[96,384]{1,0:T(8,128)}) custom-call(bf16[96,3072]{1,0:T(8,128)(2,1)} %get-tuple-element.4.low_ref, f32[96,384]{1,0:T(8,128)} %get-tuple-element.5.top_ref), custom_call_target="tpu_custom_call" | custom-call | tf_op jit(solution)/shard_map/widen/pallas_call | solution.py:798

commit v8 on v7

--- a/solution.py
+++ b/solution.py
@@ -619,22 +619,29 @@
     core_sol.start()
     store_top = pltpu.make_async_copy(top_out_v, top_out_any, local_sem.at[2])
     store_top.start()
+
+    own_half = pl.ds(pl.multiple_of(leaf * width, LANES), width)
+    other_half = pl.ds(pl.multiple_of((1 - leaf) * width, LANES), width)
+    for node in range(nodes):
+        span = pl.ds(node * width, width)
+        base[:, span] = base[:, span] - dot_t(sol_half[leaf], weighed[node * width : (node + 1) * width, own_half])
     core_sol.wait()
 
     for node in range(nodes):
         span = pl.ds(node * width, width)
         rows_here = slice(node * width, (node + 1) * width)
-        term = dot_t(sol_half[0], weighed[rows_here, :width]) + dot_t(sol_half[1], weighed[rows_here, width:])
+        term = dot_t(sol_half[1 - leaf], weighed[rows_here, other_half])
         value = (base[:, span] - term).astype(BF16)
         for piece in range(width // LANES):
             at = node * width + piece * LANES
             low_final[at // TILE, :, pl.ds(at % TILE, LANES)] = value[:, piece * LANES : (piece + 1) * LANES]
 
-    for group in range(groups):
-        for pair in range(group * group_pairs, (group + 1) * group_pairs):
+    for half in range(2):
+        for pair in range(half * pairs // 2, (half + 1) * pairs // 2):
             block = merge(low_final, choose_out[pair], high_out[pair : pair + 1], 0, None)
             store_chunks(back_send, pair * (TILE // 16), turned(block).astype(BF16))
-        start_group(back, group)
+        start_group(back, 2 * half)
+        start_group(back, 2 * half + 1)
     own_back.start()
 
     def store_out(part):

time: 65.5 us -> 63.8 us (0.974)
  Pallas kernels: 63.9 us -> 62.2 us
    pallas_call x1, Pallas kernels: 61.8 us -> 60.1 us  [shards(): pl.pallas_call(functools.partial(kernel, dims), out_shape=(jax.ShapeDtype...]
where the time goes in v8:
time: 63.8 us; the launch traced here: 62.9 us
  Pallas kernels  62.2 us (97%)
  between operations  0.64 us (1%)
    pallas_call x1, Pallas kernels, shards(): pl.pallas_call(functools.partial(kernel, dims), out_shape=(jax.ShapeDtype...  60.1 us
    pallas_call x1, Pallas kernels, shards(): pl.pallas_call(widen, grid=(2,), out_shape=(jax.ShapeDtypeStruct((sides,...  2.12 us

profile of v8, /device:TPU:0, one launch (start us, length us, event | category | flops | bytes accessed | tf_op | source)
XLA Modules:
  0.0 62.9 jit_solution(18292888645184647119)
XLA Ops:
  0.6 60.1 %substitution.1 = (bf16[96,3072]{1,0:T(8,128)(2,1)}, f32[96,384]{1,0:T(8,128)}) custom-call(s32[24,128]{1,0:T(8,128)} %bitcast.1, f32[96,3072]{1,0:T(8,128)} %drop_any.1, f32[8,384,384]{2,1,0:T(8,128)} %inverse_any.1, bf16[3072,768]{1,0:T(8,128)(2,1)} %coupling_any.1, f32[96,384]{1,0:T(8,128)} %top_sides_any.1, f32[1,384,384]{2,1,0:T(8,128)} %top_inverse_any.1, ...), custom_call_target="tpu_custom_call" | custom-call | tf_op jit(solution)/shard_map/substitution/pallas_call | solution.py:715
  60.7 2.1 %widen.1 = (f32[96,3072]{1,0:T(8,128)}, f32[96,384]{1,0:T(8,128)}) custom-call(bf16[96,3072]{1,0:T(8,128)(2,1)} %get-tuple-element.4.low_ref, f32[96,384]{1,0:T(8,128)} %get-tuple-element.5.top_ref), custom_call_target="tpu_custom_call" | custom-call | tf_op jit(solution)/shard_map/widen/pallas_call | solution.py:805

commit v9 on v8

--- a/solution.py
+++ b/solution.py
@@ -348,6 +348,60 @@
     for chunk in range(members - 1):
         ahead(chunk).start()
 
+
+    def there(chunk):
+        return pltpu.make_async_remote_copy(
+            src_ref=send_buf.at[chunk],
+            dst_ref=recv_buf.at[chunk],
+            send_sem=there_send,
+            recv_sem=there_recv.at[chunk // chunks],
+            device_id={"wide": partner(chunk)},
+            device_id_type=MESH,
+        )
+
+    def back(chunk):
+        return pltpu.make_async_remote_copy(
+            src_ref=back_send.at[chunk],
+            dst_ref=back_recv.at[chunk],
+            send_sem=back_send_sem,
+            recv_sem=back_recv_sem.at[chunk // chunks],
+            device_id={"wide": origin(chunk)},
+            device_id_type=MESH,
+        )
+
+    def start_group(copy, group):
+        last = (group + 1) * chunks
+        if group == groups - 1:
+            last -= 1
+
+        for chunk in range(group * chunks, last):
+            copy(chunk).start()
+
+    def wait_group(buf, sem, group, dst=True):
+        count = chunks - 1 if group == groups - 1 else chunks
+        part = buf.at[pl.ds(group * chunks, count)]
+        pltpu.make_async_remote_copy(
+            src_ref=part,
+            dst_ref=part,
+            send_sem=there_send,
+            recv_sem=sem.at[group],
+            device_id={"wide": me},
+            device_id_type=MESH,
+        ).wait_recv()
+
+    own_there = pltpu.make_async_copy(
+        send_buf.at[members - 1], recv_buf.at[members - 1], local_sem.at[0]
+    )
+    own_back = pltpu.make_async_copy(
+        back_send.at[members - 1], back_recv.at[members - 1], local_sem.at[1]
+    )
+
+    start_group(there, 0)
+    for group in range(1, groups):
+        pack(group)
+        start_group(there, group)
+    own_there.start()
+
     load_top.wait()
     load_tc.wait()
     core_top = pltpu.make_async_remote_copy(
@@ -369,59 +423,6 @@
     core_top.start()
     core_tc.start()
 
-    def there(chunk):
-        return pltpu.make_async_remote_copy(
-            src_ref=send_buf.at[chunk],
-            dst_ref=recv_buf.at[chunk],
-            send_sem=there_send,
-            recv_sem=there_recv.at[chunk // chunks],
-            device_id={"wide": partner(chunk)},
-            device_id_type=MESH,
-        )
-
-    def back(chunk):
-        return pltpu.make_async_remote_copy(
-            src_ref=back_send.at[chunk],
-            dst_ref=back_recv.at[chunk],
-            send_sem=back_send_sem,
-            recv_sem=back_recv_sem.at[chunk // chunks],
-            device_id={"wide": origin(chunk)},
-            device_id_type=MESH,
-        )
-
-    def start_group(copy, group):
-        last = (group + 1) * chunks
-        if group == groups - 1:
-            last -= 1
-
-        for chunk in range(group * chunks, last):
-            copy(chunk).start()
-
-    def wait_group(buf, sem, group, dst=True):
-        count = chunks - 1 if group == groups - 1 else chunks
-        part = buf.at[pl.ds(group * chunks, count)]
-        pltpu.make_async_remote_copy(
-            src_ref=part,
-            dst_ref=part,
-            send_sem=there_send,
-            recv_sem=sem.at[group],
-            device_id={"wide": me},
-            device_id_type=MESH,
-        ).wait_recv()
-
-    own_there = pltpu.make_async_copy(
-        send_buf.at[members - 1], recv_buf.at[members - 1], local_sem.at[0]
-    )
-    own_back = pltpu.make_async_copy(
-        back_send.at[members - 1], back_recv.at[members - 1], local_sem.at[1]
-    )
-
-    start_group(there, 0)
-    for group in range(1, groups):
-        pack(group)
-        start_group(there, group)
-    own_there.start()
-
     load_inverse.wait()
 
     def halves(node, _):
@@ -431,13 +432,6 @@
         return 0
 
     lax.fori_loop(0, nodes, halves, 0)
-    core_top.wait()
-    core_tc.wait()
-    for half in range(2):
-        high, low = split(top_inv_f32[half])
-        top_inv_high[half] = high
-        top_inv_low[half] = low
-
     arrived = pos_recv.at[pl.ds(0, members - 1)]
     dummy(arrived, arrived, pos_send_sem, pos_recv_sem).wait_recv()
     lane = iota((1, LANES), 1)
@@ -536,6 +530,12 @@
 
     for chunk in range(members - 1):
         send_part(chunk)
+    core_top.wait()
+    core_tc.wait()
+    for half in range(2):
+        high, low = split(top_inv_f32[half])
+        top_inv_high[half] = high
+        top_inv_low[half] = low
     make_choosers(place_ref, choose_out, high_out)
 
     def weigh(node, _):

time: 63.8 us -> 63.8 us (level); the launches traced: 62.9 us -> 63.5 us
  Pallas kernels: 62.2 us -> 62.9 us
    pallas_call x1, Pallas kernels: 60.1 us -> 60.8 us  [shards(): pl.pallas_call(functools.partial(kernel, dims), out_shape=(jax.ShapeDtype...]
where the time goes in v9:
time: 63.8 us; the launch traced here: 63.5 us
  Pallas kernels  62.9 us (99%)
  between operations  0.64 us (1%)
    pallas_call x1, Pallas kernels, shards(): pl.pallas_call(functools.partial(kernel, dims), out_shape=(jax.ShapeDtype...  60.8 us
    pallas_call x1, Pallas kernels, shards(): pl.pallas_call(widen, grid=(2,), out_shape=(jax.ShapeDtypeStruct((sides,...  2.12 us

profile of v9, /device:TPU:0, one launch (start us, length us, event | category | flops | bytes accessed | tf_op | source)
XLA Modules:
  0.0 63.5 jit_solution(16081989549646694434)
XLA Ops:
  0.6 60.8 %substitution.1 = (bf16[96,3072]{1,0:T(8,128)(2,1)}, f32[96,384]{1,0:T(8,128)}) custom-call(s32[24,128]{1,0:T(8,128)} %bitcast.1, f32[96,3072]{1,0:T(8,128)} %drop_any.1, f32[8,384,384]{2,1,0:T(8,128)} %inverse_any.1, bf16[3072,768]{1,0:T(8,128)(2,1)} %coupling_any.1, f32[96,384]{1,0:T(8,128)} %top_sides_any.1, f32[1,384,384]{2,1,0:T(8,128)} %top_inverse_any.1, ...), custom_call_target="tpu_custom_call" | custom-call | tf_op jit(solution)/shard_map/substitution/pallas_call | solution.py:715
  61.4 2.1 %widen.1 = (f32[96,3072]{1,0:T(8,128)}, f32[96,384]{1,0:T(8,128)}) custom-call(bf16[96,3072]{1,0:T(8,128)(2,1)} %get-tuple-element.4.low_ref, f32[96,384]{1,0:T(8,128)} %get-tuple-element.5.top_ref), custom_call_target="tpu_custom_call" | custom-call | tf_op jit(solution)/shard_map/widen/pallas_call | solution.py:805
